TPU v7x, 32 devices: a whole 2x2x4 slice. The times are simulated.
32 devices in a mesh: seq: 2 (over x), ctx: 4 (over z), head: 4 (over y, core).
Axes of the slice: x: 2, y: 2, z: 4, core: 2. Of those that a mesh axis runs over, the one named last changes fastest.
Arguments:
- tokens: bfloat16 [2, 2560, 1024], P('seq', 'ctx'), may hold values from -6 to 6
- doc_lengths: int32 [2, 4], P('seq'), may hold values from 80 to 1920, as said below
- norm_gains: bfloat16 [2, 1024], P(None, 'ctx'), may hold values from 0.5 to 1.5
- w_qkv: bfloat16 [3, 1024, 1024], P(None, 'ctx', 'head'), may hold values from -0.1875 to 0.1875
- w_out: bfloat16 [1024, 1024], P('head', 'ctx'), may hold values from -3 to 3
- w_in: bfloat16 [2, 1024, 2624], P(None, 'ctx', 'head'), may hold values from -0.1875 to 0.1875
- w_down: bfloat16 [2624, 1024], P('head', 'ctx'), may hold values from -0.125 to 0.125
- cotangent: bfloat16 [2, 2560, 1024], P('seq', 'ctx'), may hold values from -6 to 6
Outputs:
- out_tokens: bfloat16 [2, 2560, 1024], P('seq', 'ctx')
- grad_tokens: bfloat16 [2, 2560, 1024], P('seq', 'ctx')
- grad_gains: float32 [2, 1024], P(None, 'ctx')
- grad_qkv: float32 [3, 1024, 1024], P(None, 'ctx', 'head')
- grad_out: float32 [1024, 1024], P('head', 'ctx')
- grad_in: float32 [2, 1024, 2624], P(None, 'ctx', 'head')
- grad_down: float32 [2624, 1024], P('head', 'ctx')
Inputs may be any that keep to these rules, and one draw needn't show every extreme that they name: `doc_lengths`: each pack's 4 lengths add up to 2560. In every pack one of them, at a place drawn from the seed, is exactly the stated most, so that this document starts within the first 640 tokens and ends within the last 640; one other, also drawn from the seed, is exactly the stated least.
All inputs are finite; a program needn't handle non-finite values.
Results may differ from a plain program's by a relative error of at most 0.023.
Values may be sent and summed in bfloat16 or wider, within the bound.
A program may use at most 384 MiB of HBM per device.

v0:
```python
import jax
import jax.numpy as jnp
from jax import lax
from jax.sharding import PartitionSpec as P

HD = 64


norm_eps = 1e-05
theta_base = 160000.0
masked_score = -1e30


def passed_along(block, axis, distance):
    devices = range(lax.axis_size(axis))
    route = [((i - distance) % len(devices), i) for i in devices]
    return lax.ppermute(block, axis, route)


def token_layout(lengths, first_row, row_count):
    doc_ends = jnp.cumsum(lengths, dtype=jnp.int32)
    places = first_row + jnp.arange(row_count, dtype=jnp.int32)
    passed = places[:, None] >= doc_ends[None, :]
    doc_index = jnp.sum(passed.astype(jnp.int32), axis=1, dtype=jnp.int32)
    starts = jnp.sum(jnp.where(passed, lengths[None, :], 0), axis=1, dtype=jnp.int32)
    return (doc_index, places - starts)


def rotate(values, positions, turn_sign):
    leading = values.shape[:-1]
    head_count = values.shape[-1] // HD
    half_width = HD // 2
    frequency = theta_base ** (-(jnp.arange(half_width, dtype=jnp.float32) * (2.0 / HD)))
    angles = positions.astype(jnp.float32)[..., None] * frequency
    cosine = jnp.cos(angles)[..., None, :]
    sine_part = turn_sign * jnp.sin(angles)[..., None, :]
    shaped = values.reshape(leading + (head_count, HD))
    lower_half = shaped[..., :half_width]
    upper_half = shaped[..., half_width:]
    turned = jnp.concatenate(
        [
            lower_half * cosine - upper_half * sine_part,
            upper_half * cosine + lower_half * sine_part,
        ],
        axis=-1,
    )
    return turned.reshape(values.shape)


def layer_norm(values, gain_row):
    mean_value = jnp.mean(values, axis=-1, keepdims=True)
    centered = values - mean_value
    variance = jnp.mean(centered * centered, axis=-1, keepdims=True)
    inverse = lax.rsqrt(variance + norm_eps)
    normed = centered * inverse
    return (normed, inverse, normed * gain_row)


def norm_back(grad_scaled, normed, inverse, gain_row):
    grad_normed = grad_scaled * gain_row
    mean_grad = jnp.mean(grad_normed, axis=-1, keepdims=True)
    mean_proj = jnp.mean(grad_normed * normed, axis=-1, keepdims=True)
    grad_values = inverse * (grad_normed - mean_grad - normed * mean_proj)
    return (grad_values, jnp.sum(grad_scaled * normed, axis=0))


def exact_gelu(values):
    return jax.nn.gelu(values, approximate=False)


def back_step(
    query_part, grad_part, lse_part, delta_part, query_doc, key_part, value_part, key_doc
):
    head_count = query_part.shape[1] // HD
    query_heads = query_part.reshape(query_part.shape[0], head_count, HD)
    grad_heads = grad_part.reshape(grad_part.shape[0], head_count, HD)
    key_heads = key_part.reshape(key_part.shape[0], head_count, HD)
    value_heads = value_part.reshape(value_part.shape[0], head_count, HD)
    allowed = (query_doc[:, None] == key_doc[None, :])[None]
    scores = jnp.einsum("qhd,khd->hqk", query_heads, key_heads, preferred_element_type=jnp.float32)
    prob_rows = jnp.where(allowed, jnp.exp(scores - lse_part[:, :, None]), 0.0)
    grad_value = jnp.einsum(
        "hqk,qhd->khd",
        prob_rows.astype(jnp.bfloat16),
        grad_heads,
        preferred_element_type=jnp.float32,
    )
    grad_probs = jnp.einsum(
        "qhd,khd->hqk", grad_heads, value_heads, preferred_element_type=jnp.float32
    )
    grad_scores = (prob_rows * (grad_probs - delta_part[:, :, None])).astype(jnp.bfloat16)
    grad_query = jnp.einsum(
        "hqk,khd->qhd", grad_scores, key_heads, preferred_element_type=jnp.float32
    )
    grad_key = jnp.einsum(
        "hqk,qhd->khd", grad_scores, query_heads, preferred_element_type=jnp.float32
    )
    return (
        grad_query.reshape(query_part.shape[0], -1),
        grad_key.reshape(key_part.shape[0], -1),
        grad_value.reshape(key_part.shape[0], -1),
    )


def per_device(tokens, doc_lengths, norm_gains, w_qkv, w_out, w_in, w_down, cotangent):
    row_count = tokens.shape[1]
    hidden = tokens[0].astype(jnp.float32)
    lengths = doc_lengths[0]
    group_size = lax.axis_size("ctx")
    my_index = lax.axis_index("ctx")
    doc_here, pos_here = token_layout(lengths, my_index * row_count, row_count)
    gains_full, qkv_full, out_full, in_full, down_full = (
        lax.all_gather(norm_gains, "ctx", axis=1, tiled=True),
        lax.all_gather(w_qkv, "ctx", axis=1, tiled=True),
        lax.all_gather(w_out, "ctx", axis=1, tiled=True),
        lax.all_gather(w_in, "ctx", axis=1, tiled=True),
        lax.all_gather(w_down, "ctx", axis=1, tiled=True),
    )
    gains_float = gains_full.astype(jnp.float32)
    normed_one, inverse_one, scaled_one = layer_norm(hidden, gains_float[0])
    input_one = scaled_one.astype(jnp.bfloat16)
    raw_proj = jnp.einsum("td,cdn->tcn", input_one, qkv_full, preferred_element_type=jnp.float32)
    proj_width = raw_proj.shape[2]
    head_count = proj_width // HD
    scale_value = HD ** (-0.5)
    queries = (rotate(raw_proj[:, 0], pos_here, 1.0) * scale_value).astype(jnp.bfloat16)
    key_rows = rotate(raw_proj[:, 1], pos_here, 1.0).astype(jnp.bfloat16)
    value_rows = raw_proj[:, 2].astype(jnp.bfloat16)
    query_heads = queries.reshape(row_count, head_count, HD)
    top_score = jnp.full((head_count, row_count), masked_score, jnp.float32)
    weighted = jnp.zeros((row_count, proj_width), jnp.float32)
    key_piece = lax.all_gather(key_rows, "ctx", axis=0, tiled=True)
    value_piece = lax.all_gather(value_rows, "ctx", axis=0, tiled=True)
    piece_rows = key_piece.shape[0]
    key_doc, unused_pos = token_layout(lengths, jnp.int32(0), piece_rows)
    allowed = (doc_here[:, None] == key_doc[None, :])[None]
    scores = jnp.einsum(
        "qhd,khd->hqk",
        query_heads,
        key_piece.reshape(piece_rows, head_count, HD),
        preferred_element_type=jnp.float32,
    )
    scores = jnp.where(allowed, scores, masked_score)
    new_top = jnp.maximum(top_score, jnp.max(scores, axis=2))
    weights = jnp.where(allowed, jnp.exp(scores - new_top[:, :, None]), 0.0)
    factor = jnp.exp(top_score - new_top)
    running_sum = jnp.sum(weights, axis=2)
    update = jnp.einsum(
        "hqk,khd->qhd",
        weights.astype(jnp.bfloat16),
        value_piece.reshape(piece_rows, head_count, HD),
        preferred_element_type=jnp.float32,
    )
    weighted = weighted.reshape(row_count, head_count, HD) * factor.T[:, :, None] + update
    top_score, running_sum, weighted = (
        new_top,
        running_sum,
        weighted.reshape(row_count, proj_width),
    )
    log_total = top_score + jnp.log(running_sum)
    attn_float = (weighted.reshape(row_count, head_count, HD) / running_sum.T[:, :, None]).reshape(
        row_count, proj_width
    )
    attn_low = attn_float.astype(jnp.bfloat16)
    partial_out = jnp.dot(attn_low, out_full, preferred_element_type=jnp.float32)
    branch_one = lax.psum(partial_out.astype(jnp.bfloat16), "head").astype(jnp.float32)
    resid_one = hidden + branch_one
    normed_two, inverse_two, scaled_two = layer_norm(resid_one, gains_float[1])
    input_two = scaled_two.astype(jnp.bfloat16)
    gate_up = jnp.einsum("td,cdf->tcf", input_two, in_full, preferred_element_type=jnp.float32)
    activated, gelu_back = jax.vjp(exact_gelu, gate_up[:, 0])
    mixed_low = (activated * gate_up[:, 1]).astype(jnp.bfloat16)
    partial_ffn = jnp.dot(mixed_low, down_full, preferred_element_type=jnp.float32)
    branch_two = lax.psum(partial_ffn.astype(jnp.bfloat16), "head").astype(jnp.float32)
    result = (resid_one + branch_two).astype(jnp.bfloat16)
    gains_back, qkv_back, out_back, in_back, down_back = (
        gains_float,
        qkv_full,
        out_full,
        in_full,
        down_full,
    )
    grad_rows = cotangent[0]
    grad_down = jnp.einsum("tf,td->fd", mixed_low, grad_rows, preferred_element_type=jnp.float32)
    grad_mixed = jnp.einsum("td,fd->tf", grad_rows, down_back, preferred_element_type=jnp.float32)
    grad_gate = gelu_back(grad_mixed * gate_up[:, 1])[0]
    grad_up = grad_mixed * activated
    grad_gate_up = jnp.stack([grad_gate, grad_up], axis=1).astype(jnp.bfloat16)
    grad_in = jnp.einsum("td,tcf->cdf", input_two, grad_gate_up, preferred_element_type=jnp.float32)
    partial_two = jnp.einsum(
        "tcf,cdf->td", grad_gate_up, in_back, preferred_element_type=jnp.float32
    )
    grad_input_two = lax.psum(partial_two.astype(jnp.bfloat16), "head").astype(jnp.float32)
    grad_norm_two, gain_grad_two = norm_back(grad_input_two, normed_two, inverse_two, gains_back[1])
    grad_resid = grad_rows.astype(jnp.float32) + grad_norm_two
    grad_branch = grad_resid.astype(jnp.bfloat16)
    grad_out = jnp.einsum("tn,td->nd", attn_low, grad_branch, preferred_element_type=jnp.float32)
    grad_attn = jnp.einsum(
        "td,nd->tn", grad_branch, out_back, preferred_element_type=jnp.float32
    ).astype(jnp.bfloat16)
    delta_rows = jnp.sum(
        (grad_attn.astype(jnp.float32) * attn_float).reshape(row_count, head_count, HD), axis=2
    ).T
    zero_rows = jnp.zeros((row_count, proj_width), jnp.float32)

    def key_work(step_index, key_block, value_block, key_grad, value_grad, query_grad):
        anchor = (my_index - step_index) % group_size
        key_doc, unused_pos = token_layout(lengths, anchor * row_count, row_count)
        step_grads = back_step(
            queries, grad_attn, log_total, delta_rows, doc_here, key_block, value_block, key_doc
        )
        return (key_grad + step_grads[1], value_grad + step_grads[2], query_grad + step_grads[0])

    def send_key_grads(key_grad, value_grad):
        return (
            passed_along(key_grad.astype(jnp.bfloat16), "ctx", 1).astype(key_grad.dtype),
            passed_along(value_grad.astype(jnp.bfloat16), "ctx", 1).astype(value_grad.dtype),
        )

    def key_turn(step_index, state_now):
        key_block, value_block, key_grad, value_grad, query_grad = state_now
        key_grad, value_grad, query_grad = key_work(
            step_index, key_block, value_block, key_grad, value_grad, query_grad
        )
        key_block, value_block = passed_along((key_block, value_block), "ctx", 1)
        key_grad, value_grad = send_key_grads(key_grad, value_grad)
        return (key_block, value_block, key_grad, value_grad, query_grad)

    state_now = lax.fori_loop(
        0, group_size - 1, key_turn, (key_rows, value_rows, zero_rows, zero_rows, zero_rows)
    )
    last_grads = key_work(
        group_size - 1, state_now[0], state_now[1], state_now[2], state_now[3], state_now[4]
    )
    grad_query = last_grads[2]
    grad_key, grad_value = send_key_grads(last_grads[0], last_grads[1])
    grad_query_pre = rotate(grad_query, pos_here, -1.0) * scale_value
    grad_key_pre = rotate(grad_key, pos_here, -1.0)
    grad_raw = jnp.stack([grad_query_pre, grad_key_pre, grad_value], axis=1).astype(jnp.bfloat16)
    grad_qkv = jnp.einsum("td,tcn->cdn", input_one, grad_raw, preferred_element_type=jnp.float32)
    partial_one = jnp.einsum("tcn,cdn->td", grad_raw, qkv_back, preferred_element_type=jnp.float32)
    grad_input_one = lax.psum(partial_one.astype(jnp.bfloat16), "head").astype(jnp.float32)
    grad_norm_one, gain_grad_one = norm_back(grad_input_one, normed_one, inverse_one, gains_back[0])
    grad_tokens = (grad_resid + grad_norm_one).astype(jnp.bfloat16)
    grad_gains = jnp.stack([gain_grad_one, gain_grad_two])
    share_gains, share_qkv, share_out, share_in, share_down = (
        lax.psum_scatter(
            grad_gains.astype(jnp.bfloat16), "ctx", scatter_dimension=1, tiled=True
        ).astype(jnp.float32),
        lax.psum_scatter(
            grad_qkv.astype(jnp.bfloat16), "ctx", scatter_dimension=1, tiled=True
        ).astype(jnp.float32),
        lax.psum_scatter(
            grad_out.astype(jnp.bfloat16), "ctx", scatter_dimension=1, tiled=True
        ).astype(jnp.float32),
        lax.psum_scatter(
            grad_in.astype(jnp.bfloat16), "ctx", scatter_dimension=1, tiled=True
        ).astype(jnp.float32),
        lax.psum_scatter(
            grad_down.astype(jnp.bfloat16), "ctx", scatter_dimension=1, tiled=True
        ).astype(jnp.float32),
    )
    total_gains, total_qkv, total_out, total_in, total_down = (
        lax.psum(share_gains.astype(jnp.bfloat16), "seq").astype(jnp.float32),
        lax.psum(share_qkv.astype(jnp.bfloat16), "seq").astype(jnp.float32),
        lax.psum(share_out.astype(jnp.bfloat16), "seq").astype(jnp.float32),
        lax.psum(share_in.astype(jnp.bfloat16), "seq").astype(jnp.float32),
        lax.psum(share_down.astype(jnp.bfloat16), "seq").astype(jnp.float32),
    )
    return (
        result[None],
        grad_tokens[None],
        total_gains,
        total_qkv,
        total_out,
        total_in,
        total_down,
    )


def solution(mesh):
    return jax.shard_map(
        per_device,
        mesh=mesh,
        in_specs=(
            P("seq", "ctx", None),
            P("seq", None),
            P(None, "ctx"),
            P(None, "ctx", "head"),
            P("head", "ctx"),
            P(None, "ctx", "head"),
            P("head", "ctx"),
            P("seq", "ctx", None),
        ),
        out_specs=(
            P("seq", "ctx", None),
            P("seq", "ctx", None),
            P(None, "ctx"),
            P(None, "ctx", "head"),
            P("head", "ctx"),
            P(None, "ctx", "head"),
            P("head", "ctx"),
        ),
        check_vma=False,
    )
```

profile of v0, /device:TPU:0, one launch (start us, length us, event | category | flops | bytes accessed | tf_op | source)
XLA Modules:
  0.0 738.2 jit_solution(5091107275937894838)
XLA Ops:
  7.2 2.0 copy.31
  10.2 12.9 %all_gather.21 = bf16[2,1024]{1,0:T(2,128)(2,1)S(1)} all-gather(bf16[2,256]{1,0:T(2,128)(2,1)} %param.12), channel_id=1, replica_groups=mesh['seq'=2,'ctx'=4,'head'=4] {'ctx'}, dimensions={1}, use_global_device_ids=true | all-gather | bytes 5120 | tf_op jit(solution)/shard_map/all_gather | solution.py:113
  23.8 1.6 convert_reduce_fusion.1
  26.3 24.3 %all-gather.7.cloned.1.call-done = bf16[3,1024,256]{1,2,0:T(8,128)(2,1)} async-done(((bf16[3,256,256]{1,2,0:T(8,128)(2,1)}), bf16[3,1024,256]{1,2,0:T(8,128)(2,1)}) %all-gather.7.cloned.1.call-update) | async-done | bytes 1572880 | tf_op jit(solution)/shard_map/all_gather | solution.py:114
  50.6 2.9 fusion.148
  57.3 20.3 %all_gather.25 = bf16[256,1024]{1,0:T(8,128)(2,1)} all-gather(bf16[256,256]{1,0:T(8,128)(2,1)} %param.14), channel_id=1, replica_groups=mesh['seq'=2,'ctx'=4,'head'=4] {'ctx'}, dimensions={1}, use_global_device_ids=true | all-gather | bytes 655360 | tf_op jit(solution)/shard_map/all_gather | solution.py:115
  78.6 12.8 %all-gather.9.cloned.1.call-done = bf16[2560,256]{0,1:T(8,128)(2,1)} async-done(((bf16[640,256]{0,1:T(8,128)(2,1)}), bf16[2560,256]{0,1:T(8,128)(2,1)}) %all-gather.9.cloned.1.call-update) | async-done | bytes 1310736 | tf_op jit(solution)/shard_map/all_gather | solution.py:132
  91.4 14.4 %select_reduce_fusion = (f32[4,640]{1,0:T(4,128)S(1)}, f32[4,640,2560]{2,1,0:T(8,128)}) fusion(pred[640,2560]{1,0:T(8,128)(4,1)S(1)} %broadcast_compare_fusion.1, bf16[640,4,64]{0,2,1:T(8,128)(2,1)S(1)} %fusion.99, bf16[2560,4,64]{0,2,1:T(8,128)(2,1)} %bitcast.337), kind=kOutput, calls=%fused_computation.17 | convolution fusion | flops 851965440 | bytes 29501440 | tf_op jit(solution)/shard_map/qhd,khd->hqk/dot_general | solution.py:137
  105.8 13.3 %fusion.9 = f32[4,640]{1,0:T(4,128)S(1)} fusion(f32[4,640,2560]{2,1,0:T(8,128)} %get-tuple-element.457, f32[4,640]{1,0:T(4,128)S(1)} %broadcast_maximum_fusion, pred[640,2560]{1,0:T(8,128)(4,1)S(1)} %broadcast_compare_fusion.1), kind=kLoop, calls=%fused_computation.18 | loop fusion | flops 26211840 | bytes 27873280 | tf_op jit(solution)/shard_map/reduce_sum | solution.py:147
  119.1 7.2 all-gather.15.cloned.1.call-done
  126.3 13.0 %fusion.91 = f32[640,4,64]{0,2,1:T(8,128)S(1)} fusion(bf16[2560,4,64]{0,2,1:T(8,128)(2,1)} %bitcast.366, f32[4,640,2560]{2,1,0:T(8,128)} %get-tuple-element.457, f32[4,640]{1,0:T(4,128)S(1)} %broadcast_maximum_fusion, pred[640,2560]{1,0:T(8,128)(4,1)S(1)} %broadcast_compare_fusion.1, f32[640,4]{0,1:T(4,128)S(1)} %bitcast.351, ...), kind=kOutput, calls=%fused_computation.137 | convolution fusion | flops 865402880 | bytes 29849600 | tf_op jit(solution)/shard_map/hqk,khd->qhd/dot_general | solution.py:148
  141.0 1.6 convolution_convert_fusion.2
  143.4 17.8 %all-gather.13.cloned.1.call-done = bf16[656,1024]{1,0:T(8,128)(2,1)} async-done(((bf16[656,256]{1,0:T(8,128)(2,1)}), bf16[656,1024]{1,0:T(8,128)(2,1)}) %all-gather.13.cloned.1.call-update) | async-done | bytes 1343504 | tf_op jit(solution)/shard_map/all_gather | solution.py:117
  161.2 3.8 fusion.83
  165.0 36.4 %all-reduce.7.cloned.1.call-done = bf16[640,1024]{1,0:T(8,128)(2,1)} async-done(((bf16[640,1024]{1,0:T(8,128)(2,1)}), bf16[640,1024]{1,0:T(8,128)(2,1)}) %all-reduce.7.cloned.1.call-update) | async-done | bytes 1310736 | tf_op jit(solution)/shard_map/psum | solution.py:166
  201.4 1.8 fusion.45
  203.9 54.9 %all-gather.11.cloned.1.call-done = bf16[2,1024,656]{1,2,0:T(8,128)(2,1)} async-done(((bf16[2,256,656]{1,2,0:T(8,128)(2,1)}), bf16[2,1024,656]{1,2,0:T(8,128)(2,1)}) %all-gather.11.cloned.1.call-update) | async-done | bytes 2686992 | tf_op jit(solution)/shard_map/all_gather | solution.py:116
  258.8 4.3 fusion.105
  263.2 4.1 fusion.98
  270.3 3.3 bitcast_convert_fusion.1
  276.0 5.4 convolution_convert_fusion.3
  281.4 29.5 %all-reduce.9.cloned.1.call-done = bf16[640,1024]{1,0:T(8,128)(2,1)} async-done(((bf16[640,1024]{1,0:T(8,128)(2,1)}), bf16[640,1024]{1,0:T(8,128)(2,1)}) %all-reduce.9.cloned.1.call-update) | async-done | bytes 1310736 | tf_op jit(solution)/shard_map/psum | solution.py:193
  310.9 2.8 fusion.42
  313.8 1.8 fusion.40
  317.5 100.4 %while.24 = (s32[]{:T(128)}, bf16[640,256]{0,1:T(8,128)(2,1)S(1)}, bf16[640,256]{0,1:T(8,128)(2,1)S(1)}, f32[640,256]{0,1:T(8,128)S(1)}, f32[640,256]{0,1:T(8,12...) while((s32[]{:T(128)}, bf16[640,256]{0,1:T(8,128)(2,1)S(1)}, ...), condition=%wide.region_19.20_spmd.clone, body=%wide.region_17.19_spmd.clone.sunk | while | flops 1063738880 | bytes 52718620 | solution.py:229
  317.6 1.5 collective-permute-start
  322.8 4.1 multiply_convert_fusion.5
  334.8 9.4 %collective-permute-done.2 = bf16[640,256]{0,1:T(8,128)(2,1)} collective-permute-done((bf16[640,256]{0,1:T(8,128)(2,1)}, bf16[640,256]{0,1:T(8,128)(2,1)}, u32[]{:S(2)}, u32[]{:S(2)}) %collective-permute-start.2) | collective-permute-done | bytes 327712 | tf_op jit(solution)/shard_map/while/body/eval_jaxpr/ppermute | solution.py:17
  345.2 4.9 collective-permute-done.3
  350.0 1.9 convert_element_type.492
  355.4 4.1 multiply_convert_fusion.5
  364.7 2.3 collective-permute-start.3
  368.2 2.0 bitcast_add_fusion.6
  370.2 8.4 %collective-permute-done.2 = bf16[640,256]{0,1:T(8,128)(2,1)} collective-permute-done((bf16[640,256]{0,1:T(8,128)(2,1)}, bf16[640,256]{0,1:T(8,128)(2,1)}, u32[]{:S(2)}, u32[]{:S(2)}) %collective-permute-start.2) | collective-permute-done | bytes 327712 | tf_op jit(solution)/shard_map/while/body/eval_jaxpr/ppermute | solution.py:17
  379.6 3.9 collective-permute-done.3
  383.5 1.9 convert_element_type.492
  387.7 4.1 multiply_convert_fusion.5
  396.4 4.1 collective-permute-start.3
  401.7 2.0 bitcast_add_fusion.6
  403.7 8.4 %collective-permute-done.2 = bf16[640,256]{0,1:T(8,128)(2,1)} collective-permute-done((bf16[640,256]{0,1:T(8,128)(2,1)}, bf16[640,256]{0,1:T(8,128)(2,1)}, u32[]{:S(2)}, u32[]{:S(2)}) %collective-permute-start.2) | collective-permute-done | bytes 327712 | tf_op jit(solution)/shard_map/while/body/eval_jaxpr/ppermute | solution.py:17
  413.1 3.0 collective-permute-done.3
  416.1 1.9 convert_element_type.492
  419.1 2.5 multiply_convert_fusion.1
  422.2 2.0 fusion.157
  424.2 2.3 fusion.15
  426.7 2.2 copy.33
  432.7 5.3 collective-permute-done.4
  438.7 3.8 collective-permute-done.5
  442.6 3.8 bitcast_convert_fusion
  447.3 3.1 convolution_convert_fusion.4
  450.6 7.5 %convolution_convert_fusion.1 = bf16[656,1024]{1,0:T(8,128)(2,1)} fusion(bf16[1,640,1024]{2,1,0:T(8,128)(2,1)S(1)} %copy-done.22, f32[640,2,656]{0,2,1:T(8,128)} %copy-done.9), kind=kOutput, calls=%fused_computation.121 | convolution fusion | flops 888213504 | bytes 6012928 | tf_op jit(solution)/shard_map/tf,td->fd/dot_general | solution.py:184
  458.2 4.1 fusion.77
  462.3 5.1 convert_bitcast_fusion.1
  467.5 36.8 %all-reduce.11.cloned.1.call-done = (bf16[640,1024]{1,0:T(8,128)(2,1)}, bf16[640,1024]{1,0:T(8,128)(2,1)}) async-done(((bf16[640,1024]{1,0:T(8,128)(2,1)}, bf16[640,1024]{1,0:T(8,128)(2,1)}), (bf16[640,1024]{1,0:T(8,128)(2,1)}, bf16[640,1024]{1,0:T(8,128)(2,1)})) %all-reduce.11.cloned.1.call-update) | async-done | bytes 2621456 | tf_op jit(solution)/shard_map/psum | solution.py:174
  504.3 2.5 fusion.44
  507.8 21.1 %reduce-scatter.10.cloned.1.call-done = bf16[256,256]{1,0:T(8,128)(2,1)} async-done(((bf16[256,1024]{1,0:T(8,128)(2,1)}), bf16[256,256]{1,0:T(8,128)(2,1)}) %reduce-scatter.10.cloned.1.call-update) | async-done | bytes 131088 | tf_op jit(solution)/shard_map/reduce_scatter | solution.py:253
  528.9 32.7 %reduce-scatter.14.cloned.1.call-done = bf16[656,256]{1,0:T(8,128)(2,1)} async-done(((bf16[656,1024]{1,0:T(8,128)(2,1)}), bf16[656,256]{1,0:T(8,128)(2,1)}) %reduce-scatter.14.cloned.1.call-update) | async-done | bytes 335888 | tf_op jit(solution)/shard_map/reduce_scatter | solution.py:259
  561.7 36.5 %reduce-scatter.8.cloned.1.call-done = bf16[3,256,256]{1,2,0:T(8,128)(2,1)} async-done(((bf16[3,1024,256]{1,2,0:T(8,128)(2,1)}), bf16[3,256,256]{1,2,0:T(8,128)(2,1)}) %reduce-scatter.8.cloned.1.call-update) | async-done | bytes 393232 | tf_op jit(solution)/shard_map/reduce_scatter | solution.py:250
  598.1 54.3 %reduce-scatter.12.cloned.1.call-done = bf16[2,256,656]{1,2,0:T(8,128)(2,1)} async-done(((bf16[2,1024,656]{1,2,0:T(8,128)(2,1)}), bf16[2,256,656]{1,2,0:T(8,128)(2,1)}) %reduce-scatter.12.cloned.1.call-update) | async-done | bytes 671760 | tf_op jit(solution)/shard_map/reduce_scatter | solution.py:256
  652.4 4.2 fusion.80
  656.6 18.1 %reduce-scatter.16.cloned.1.call-done = bf16[256,2]{1,0:T(8,128)(2,1)} async-done(((bf16[1024,2]{1,0:T(8,128)(2,1)}), bf16[256,2]{1,0:T(8,128)(2,1)}) %reduce-scatter.16.cloned.1.call-update) | async-done | bytes 1040
  675.6 4.9 psum.67
  681.2 45.3 %all-reduce.13.cloned.1.call-done = (bf16[3,256,256]{1,2,0:T(8,128)(2,1)}, bf16[256,256]{1,0:T(8,128)(2,1)}, bf16[2,256,656]{1,2,0:T(8,128)(2,1)}, bf16[656,256]{1,0:T(8,128)(2,1)}) async-done(((bf16[3,256,256]{1,2,0:T(8,128)(2,1)}, bf16[256,256]{1,0:T(8,128)(2,1)}, bf16[2,256,656]{1,2,0:T(8,128)(2,1)}, bf16[656,256]{1,0:T(8,128)(2,1)}), (bf16[3,256,256]{1,2,0:T(8,128)(2,1)}, bf16[256,256]{1,0:T(8,128)(2,1)}, ...) | async-done | bytes 1531920 | tf_op jit(solution)/shard_map/psum | solution.py:265
  726.5 2.3 convert_element_type.277
  (236 shorter events, 62.6 us)
Async XLA Ops:
  7.2 18.2 %copy-start = (bf16[1,640,1024]{2,1,0:T(8,128)(2,1)S(1)}, bf16[1,640,1024]{2,1,0:T(8,128)(2,1)}, u32[]{:S(2)}) copy-start(bf16[1,640,1024]{2,1,0:T(8,128)(2,1)} %param.10) | copy-start | bytes 3932164
  7.2 43.4 %all-gather.7.cloned.1.call-start = ((), (), s32[]{:S(2)}) async-start(), calls=%async_computation.5 | async-start | bytes 1966080 | tf_op jit(solution)/shard_map/all_gather | solution.py:114
  9.3 82.1 %all-gather.9.cloned.1.call-start = ((), (), s32[]{:S(2)}) async-start(), calls=%async_computation.6 | async-start | bytes 1638400 | tf_op jit(solution)/shard_map/all_gather | solution.py:132
  25.4 28.2 %copy-start.36 = (f32[640]{0:T(1024)}, f32[640]{0:T(1024)S(1)}, u32[]{:S(2)}) copy-start(f32[640]{0:T(1024)S(1)} %broadcast_multiply_fusion.6) | copy-start | bytes 7684
  25.9 27.7 %copy-start.38 = (f32[640]{0:T(1024)}, f32[640]{0:T(1024)S(1)}, u32[]{:S(2)}) copy-start(f32[640]{0:T(1024)S(1)} %add_rsqrt_fusion.1) | copy-start | bytes 7684
  25.9 27.6 %copy-start.40 = (f32[1,1024]{1,0:T(1,128)}, f32[1,1024]{1,0:T(1,128)S(1)}, u32[]{:S(2)}) copy-start(f32[1,1024]{1,0:T(1,128)S(1)} %get-tuple-element.454) | copy-start | bytes 12292
  53.6 2.2 copy-start.19
  55.7 70.7 %all-gather.15.cloned.1.call-start = ((), (), s32[]{:S(2)}) async-start(), calls=%async_computation.15 | async-start | bytes 1638400 | tf_op jit(solution)/shard_map/all_gather | solution.py:133
  56.5 104.7 %all-gather.13.cloned.1.call-start = ((), (), s32[]{:S(2)}) async-start(), calls=%async_computation.9 | async-start | bytes 1679360 | tf_op jit(solution)/shard_map/all_gather | solution.py:117
  57.1 144.3 %all-reduce.7.cloned.1.call-start = ((), (), s32[]{:S(2)}) async-start(), calls=%async_computation.7 | async-start | bytes 2621440 | tf_op jit(solution)/shard_map/psum | solution.py:166
  57.1 21.4 %copy-start.23 = (f32[640,4,32]{0,2,1:T(8,128)S(1)}, f32[640,4,32]{0,2,1:T(8,128)}, u32[]{:S(2)}) copy-start(f32[640,4,32]{0,2,1:T(8,128)} %get-tuple-element.447) | copy-start | bytes 983044
  57.1 21.4 %copy-start.24 = (f32[640,4,32]{0,2,1:T(8,128)S(1)}, f32[640,4,32]{0,2,1:T(8,128)}, u32[]{:S(2)}) copy-start(f32[640,4,32]{0,2,1:T(8,128)} %get-tuple-element.448) | copy-start | bytes 983044
  126.3 14.6 %copy-start.13 = (bf16[256,1024]{1,0:T(8,128)(2,1)S(1)}, bf16[256,1024]{1,0:T(8,128)(2,1)}, u32[]{:S(2)}) copy-start(bf16[256,1024]{1,0:T(8,128)(2,1)} %all_gather.25) | copy-start | bytes 1572868
  141.0 20.3 %copy-start.20 = (bf16[1,640,1024]{2,1,0:T(8,128)(2,1)S(1)}, bf16[1,640,1024]{2,1,0:T(8,128)(2,1)}, u32[]{:S(2)}) copy-start(bf16[1,640,1024]{2,1,0:T(8,128)(2,1)} %param.17) | copy-start | bytes 3932164
  142.6 116.3 %all-gather.11.cloned.1.call-start = ((), (), s32[]{:S(2)}) async-start(), calls=%async_computation.8 | async-start | bytes 3358720 | tf_op jit(solution)/shard_map/all_gather | solution.py:116
  143.1 167.8 %all-reduce.9.cloned.1.call-start = ((), (), s32[]{:S(2)}) async-start(), calls=%async_computation.10 | async-start | bytes 2621440 | tf_op jit(solution)/shard_map/psum | solution.py:193
  201.4 1.8 copy-start.2
  258.8 4.4 copy-start.11
  263.2 4.1 copy-start.9
  267.3 3.0 copy-start.43
  273.6 230.7 %all-reduce.11.cloned.1.call-start = ((), (), s32[]{:S(2)}) async-start(), calls=%async_computation.17 | async-start | bytes 5242880 | tf_op jit(solution)/shard_map/psum | solution.py:174
  310.9 2.8 copy-start.12
  310.9 2.8 copy-start.21
  313.8 1.8 copy-start.14
  313.8 1.8 copy-start.18
  315.6 1.6 copy-start.1
  315.6 1.9 copy-start.5
  317.6 34.3 %collective-permute-start = (bf16[640,256]{0,1:T(8,128)(2,1)S(1)}, bf16[640,256]{0,1:T(8,128)(2,1)S(1)}, u32[]{:S(2)}, u32[]{:S(2)}) collective-permute-start(bf16[640,256]{0,1:T(8,128)(2,1)S(1)} %copy.52), channel_id=1, source_target_pairs={{12,0},{0,4},{4,8},{8,12},{13,1},{1,5},{5,9},{9,13},{14,2},{2,6},{... | collective-permute-start | bytes 983048 | tf_op jit(solution)/shard_map/while/body/eval_jaxpr/ppermute | solution.py:17
  319.8 32.1 %collective-permute-start.1 = (bf16[640,256]{0,1:T(8,128)(2,1)}, bf16[640,256]{0,1:T(8,128)(2,1)S(1)}, u32[]{:S(2)}, u32[]{:S(2)}) collective-permute-start(bf16[640,256]{0,1:T(8,128)(2,1)} %copy.53), channel_id=1, source_target_pairs={{12,0},{0,4},{4,8},{8,12},{13,1},{1,5},{5,9},{9,13},{14,2},{2,6},{... | collective-permute-start | bytes 983048 | tf_op jit(solution)/shard_map/while/body/eval_jaxpr/ppermute | solution.py:17
  328.4 3.0 copy-start.6
  328.4 15.8 %collective-permute-start.2 = (bf16[640,256]{0,1:T(8,128)(2,1)}, bf16[640,256]{0,1:T(8,128)(2,1)}, u32[]{:S(2)}, u32[]{:S(2)}) collective-permute-start(bf16[640,256]{0,1:T(8,128)(2,1)} %fusion.218), channel_id=1, source_target_pairs={{12,0},{0,4},{4,8},{8,12},{13,1},{1,5},{5,9},{9,13},{14,2},{2,6},{... | collective-permute-start | bytes 983048 | tf_op jit(solution)/shard_map/while/body/eval_jaxpr/ppermute | solution.py:17
  332.2 17.9 %collective-permute-start.3 = (bf16[640,256]{0,1:T(8,128)(2,1)}, bf16[640,256]{0,1:T(8,128)(2,1)}, u32[]{:S(2)}, u32[]{:S(2)}) collective-permute-start(bf16[640,256]{0,1:T(8,128)(2,1)} %fusion.220), channel_id=1, source_target_pairs={{12,0},{0,4},{4,8},{8,12},{13,1},{1,5},{5,9},{9,13},{14,2},{2,6},{... | collective-permute-start | bytes 983048 | tf_op jit(solution)/shard_map/while/body/eval_jaxpr/ppermute | solution.py:17
  351.9 33.5 %collective-permute-start = (bf16[640,256]{0,1:T(8,128)(2,1)S(1)}, bf16[640,256]{0,1:T(8,128)(2,1)S(1)}, u32[]{:S(2)}, u32[]{:S(2)}) collective-permute-start(bf16[640,256]{0,1:T(8,128)(2,1)S(1)} %copy.52), channel_id=1, source_target_pairs={{12,0},{0,4},{4,8},{8,12},{13,1},{1,5},{5,9},{9,13},{14,2},{2,6},{... | collective-permute-start | bytes 983048 | tf_op jit(solution)/shard_map/while/body/eval_jaxpr/ppermute | solution.py:17
  352.7 32.7 %collective-permute-start.1 = (bf16[640,256]{0,1:T(8,128)(2,1)}, bf16[640,256]{0,1:T(8,128)(2,1)S(1)}, u32[]{:S(2)}, u32[]{:S(2)}) collective-permute-start(bf16[640,256]{0,1:T(8,128)(2,1)} %copy.53), channel_id=1, source_target_pairs={{12,0},{0,4},{4,8},{8,12},{13,1},{1,5},{5,9},{9,13},{14,2},{2,6},{... | collective-permute-start | bytes 983048 | tf_op jit(solution)/shard_map/while/body/eval_jaxpr/ppermute | solution.py:17
  360.9 3.0 copy-start.6
  360.9 17.6 %collective-permute-start.2 = (bf16[640,256]{0,1:T(8,128)(2,1)}, bf16[640,256]{0,1:T(8,128)(2,1)}, u32[]{:S(2)}, u32[]{:S(2)}) collective-permute-start(bf16[640,256]{0,1:T(8,128)(2,1)} %fusion.218), channel_id=1, source_target_pairs={{12,0},{0,4},{4,8},{8,12},{13,1},{1,5},{5,9},{9,13},{14,2},{2,6},{... | collective-permute-start | bytes 983048 | tf_op jit(solution)/shard_map/while/body/eval_jaxpr/ppermute | solution.py:17
  364.7 18.8 %collective-permute-start.3 = (bf16[640,256]{0,1:T(8,128)(2,1)}, bf16[640,256]{0,1:T(8,128)(2,1)}, u32[]{:S(2)}, u32[]{:S(2)}) collective-permute-start(bf16[640,256]{0,1:T(8,128)(2,1)} %fusion.220), channel_id=1, source_target_pairs={{12,0},{0,4},{4,8},{8,12},{13,1},{1,5},{5,9},{9,13},{14,2},{2,6},{... | collective-permute-start | bytes 983048 | tf_op jit(solution)/shard_map/while/body/eval_jaxpr/ppermute | solution.py:17
  385.4 32.5 %collective-permute-start = (bf16[640,256]{0,1:T(8,128)(2,1)S(1)}, bf16[640,256]{0,1:T(8,128)(2,1)S(1)}, u32[]{:S(2)}, u32[]{:S(2)}) collective-permute-start(bf16[640,256]{0,1:T(8,128)(2,1)S(1)} %copy.52), channel_id=1, source_target_pairs={{12,0},{0,4},{4,8},{8,12},{13,1},{1,5},{5,9},{9,13},{14,2},{2,6},{... | collective-permute-start | bytes 983048 | tf_op jit(solution)/shard_map/while/body/eval_jaxpr/ppermute | solution.py:17
  386.2 31.7 %collective-permute-start.1 = (bf16[640,256]{0,1:T(8,128)(2,1)}, bf16[640,256]{0,1:T(8,128)(2,1)S(1)}, u32[]{:S(2)}, u32[]{:S(2)}) collective-permute-start(bf16[640,256]{0,1:T(8,128)(2,1)} %copy.53), channel_id=1, source_target_pairs={{12,0},{0,4},{4,8},{8,12},{13,1},{1,5},{5,9},{9,13},{14,2},{2,6},{... | collective-permute-start | bytes 983048 | tf_op jit(solution)/shard_map/while/body/eval_jaxpr/ppermute | solution.py:17
  393.3 2.3 copy-start.6
  393.3 18.8 %collective-permute-start.2 = (bf16[640,256]{0,1:T(8,128)(2,1)}, bf16[640,256]{0,1:T(8,128)(2,1)}, u32[]{:S(2)}, u32[]{:S(2)}) collective-permute-start(bf16[640,256]{0,1:T(8,128)(2,1)} %fusion.218), channel_id=1, source_target_pairs={{12,0},{0,4},{4,8},{8,12},{13,1},{1,5},{5,9},{9,13},{14,2},{2,6},{... | collective-permute-start | bytes 983048 | tf_op jit(solution)/shard_map/while/body/eval_jaxpr/ppermute | solution.py:17
  396.4 19.7 %collective-permute-start.3 = (bf16[640,256]{0,1:T(8,128)(2,1)}, bf16[640,256]{0,1:T(8,128)(2,1)}, u32[]{:S(2)}, u32[]{:S(2)}) collective-permute-start(bf16[640,256]{0,1:T(8,128)(2,1)} %fusion.220), channel_id=1, source_target_pairs={{12,0},{0,4},{4,8},{8,12},{13,1},{1,5},{5,9},{9,13},{14,2},{2,6},{... | collective-permute-start | bytes 983048 | tf_op jit(solution)/shard_map/while/body/eval_jaxpr/ppermute | solution.py:17
  426.5 2.4 copy-start.7
  426.6 11.4 %collective-permute-start.4 = (bf16[640,256]{0,1:T(8,128)(2,1)S(1)}, bf16[640,256]{0,1:T(8,128)(2,1)S(1)}, u32[]{:S(2)}, u32[]{:S(2)}) collective-permute-start(bf16[640,256]{0,1:T(8,128)(2,1)S(1)} %fusion.101), channel_id=1, source_target_pairs={{12,0},{0,4},{4,8},{8,12},{13,1},{1,5},{5,9},{9,13},{14,2},{2,6},{... | collective-permute-start | bytes 983048 | tf_op jit(solution)/shard_map/ppermute | solution.py:17
  428.9 2.7 copy-start.8
  431.3 11.3 %collective-permute-start.5 = (bf16[640,256]{1,0:T(8,128)(2,1)S(1)}, bf16[640,256]{1,0:T(8,128)(2,1)S(1)}, u32[]{:S(2)}, u32[]{:S(2)}) collective-permute-start(bf16[640,256]{1,0:T(8,128)(2,1)S(1)} %add_convert_fusion.1), channel_id=1, source_target_pairs={{12,0},{0,4},{4,8},{8,12},{13,1},{1,5},{5,9},{9,13},{14,2},{2,6},{... | collective-permute-start | bytes 983048 | tf_op jit(solution)/shard_map/ppermute | solution.py:17
  438.5 7.9 %copy-start.33 = (bf16[640,1,256]{2,0,1:T(8,128)(2,1)}, bf16[640,1,256]{2,0,1:T(8,128)(2,1)S(1)}, u32[]{:S(2)}) copy-start(bf16[640,1,256]{2,0,1:T(8,128)(2,1)S(1)} %copy.34) | copy-start | bytes 983044
  438.7 7.6 %copy-start.34 = (bf16[640,1,256]{2,0,1:T(8,128)(2,1)}, bf16[640,1,256]{2,0,1:T(8,128)(2,1)S(1)}, u32[]{:S(2)}) copy-start(bf16[640,1,256]{2,0,1:T(8,128)(2,1)S(1)} %copy.35) | copy-start | bytes 983044
  442.6 3.8 copy-start.44
  446.4 4.2 copy-start.22
  446.4 82.5 %reduce-scatter.10.cloned.1.call-start = ((), (), s32[]{:S(2)}) async-start(), calls=%async_computation.12 | async-start | bytes 655360 | tf_op jit(solution)/shard_map/reduce_scatter | solution.py:253
  450.5 7.7 %copy-start.37 = (f32[640]{0:T(1024)S(1)}, f32[640]{0:T(1024)}, u32[]{:S(2)}) copy-start(f32[640]{0:T(1024)} %copy-done.36) | copy-start | bytes 7684
  450.5 7.7 %copy-start.39 = (f32[640]{0:T(1024)S(1)}, f32[640]{0:T(1024)}, u32[]{:S(2)}) copy-start(f32[640]{0:T(1024)} %copy-done.38) | copy-start | bytes 7684
  450.5 7.7 %copy-start.41 = (f32[1,1024]{1,0:T(1,128)S(1)}, f32[1,1024]{1,0:T(1,128)}, u32[]{:S(2)}) copy-start(f32[1,1024]{1,0:T(1,128)} %copy-done.40) | copy-start | bytes 12292
  450.5 111.2 %reduce-scatter.14.cloned.1.call-start = ((), (), s32[]{:S(2)}) async-start(), calls=%async_computation.14 | async-start | bytes 1679360 | tf_op jit(solution)/shard_map/reduce_scatter | solution.py:259
  458.1 4.3 copy-start.3
  458.1 4.3 copy-start.26
  458.1 140.0 %reduce-scatter.8.cloned.1.call-start = ((), (), s32[]{:S(2)}) async-start(), calls=%async_computation.11 | async-start | bytes 1966080 | tf_op jit(solution)/shard_map/reduce_scatter | solution.py:250
  462.3 190.1 %reduce-scatter.12.cloned.1.call-start = ((), (), s32[]{:S(2)}) async-start(), calls=%async_computation.13 | async-start | bytes 3358720 | tf_op jit(solution)/shard_map/reduce_scatter | solution.py:256
  467.4 207.3 %reduce-scatter.16.cloned.1.call-start = ((), (), s32[]{:S(2)}) async-start(), calls=%async_computation.16 | async-start | bytes 327680
  507.8 218.7 %all-reduce.13.cloned.1.call-start = ((), (), s32[]{:S(2)}) async-start(), calls=%async_computation.18 | async-start | bytes 3063808 | tf_op jit(solution)/shard_map/psum | solution.py:265
  726.5 2.3 copy-start.29
  726.5 3.4 copy-start.30
  726.5 4.3 copy-start.35
  (13 other events, 14.3 us)
Sparse Core Ops, SparseCore 0:
  10.1 40.3 all-gather.6
  55.8 35.5 all-gather.8
  93.6 32.7 all-gather.14
  127.7 33.4 all-gather.12
  164.0 37.3 all-reduce.6
  202.8 55.9 all-gather.10
  273.7 37.1 all-reduce.8
  446.5 57.7 all-reduce.10
  507.2 21.6 reduce-scatter.9
  531.7 29.9 reduce-scatter.13
  564.0 34.0 reduce-scatter.7
  600.3 52.0 reduce-scatter.11
  655.3 19.3 reduce-scatter.15
  677.1 49.3 all-reduce.12
where the time goes:
time: 748 us; the launch traced here: 738 us
  waiting for transfers between devices  476 us (64%)
  matrix products  107 us (14%)
  other arithmetic  66.9 us (9%)
  blocking collectives  38.1 us (5%)
  local copies, waits for them, and re-layouts  18.5 us (2%)
  starting transfers between devices  16.1 us (2%)
  between operations  14.8 us (2%)
    all_gather x1, waiting for transfers between devices, per_device(): lax.all_gather(w_in, 'ctx', axis=1, tiled=True)  54.9 us
    reduce_scatter x1, waiting for transfers between devices, per_device(): lax.psum_scatter(grad_in.astype(jnp.bfloat16), 'ctx', scatter_dimension=1...  54.3 us
    ppermute x14, waiting for transfers between devices, passed_along(): return lax.ppermute(block, axis, route)  47.1 us
    psum x1, waiting for transfers between devices, per_device(): lax.psum(share_qkv.astype(jnp.bfloat16), 'seq').astype(jnp.float32)  45.3 us
    psum x1, waiting for transfers between devices, per_device(): lax.psum(partial_ffn.astype(jnp.bfloat16), 'head').astype(jnp.float32)  36.8 us
    reduce_scatter x1, waiting for transfers between devices, per_device(): lax.psum_scatter(grad_qkv.astype(jnp.bfloat16), 'ctx', scatter_dimension=...  36.5 us
    psum x1, waiting for transfers between devices, per_device(): lax.psum(partial_out.astype(jnp.bfloat16), 'head').astype(jnp.float32)  36.4 us
    reduce_scatter x1, waiting for transfers between devices, per_device(): lax.psum_scatter(grad_down.astype(jnp.bfloat16), 'ctx', scatter_dimension...  32.7 us
  transfers between devices with their start and end apart: 28, of which 22 were waited for; matrix products, arithmetic and copies ran while one was open for 20% of the time, Pallas kernels for 0%

commit v1 on v0

--- a/solution.py
+++ b/solution.py
@@ -102,7 +102,7 @@
     )
 
 
-def per_device(tokens, doc_lengths, norm_gains, w_qkv, w_out, w_in, w_down, cotangent):
+def per_device_ring(tokens, doc_lengths, norm_gains, w_qkv, w_out, w_in, w_down, cotangent):
     row_count = tokens.shape[1]
     hidden = tokens[0].astype(jnp.float32)
     lengths = doc_lengths[0]
@@ -278,9 +278,242 @@
     )
 
 
+def pair_swap(block, axis, mask):
+    size = lax.axis_size(axis)
+    return lax.ppermute(block, axis, [(i, i ^ mask) for i in range(size)])
+
+
+def gather_weight(weight, dim):
+    half = weight.shape[dim] // lax.axis_size("seq")
+    mine = lax.dynamic_slice_in_dim(weight, lax.axis_index("seq") * half, half, dim)
+    return lax.all_gather(mine, ("ctx", "seq"), axis=dim, tiled=True)
+
+
+def gather_gains(gains):
+    group = lax.axis_size("ctx")
+    if group > 4:
+        return lax.all_gather(gains, "ctx", axis=1, tiled=True)
+    me = lax.axis_index("ctx")
+    width = gains.shape[1]
+    full = jnp.zeros((gains.shape[0], width * group), gains.dtype)
+    for k in range(group):
+        block = gains if k == 0 else passed_along(gains, "ctx", k)
+        full = lax.dynamic_update_slice_in_dim(full, block, ((me - k) % group) * width, 1)
+    return full
+
+
+def reduce_weight(grad):
+    return lax.psum_scatter(grad, ("ctx", "seq"), scatter_dimension=1, tiled=True)
+
+
+def reduce_weight_rows(share):
+    other = pair_swap(share, "seq", 1)
+    first = lax.axis_index("seq") == 0
+    low_part = jnp.where(first, share, other)
+    high_part = jnp.where(first, other, share)
+    return jnp.concatenate([low_part, high_part], axis=1).astype(jnp.float32)
+
+
+def reduce_gains(grads):
+    group = lax.axis_size("ctx")
+    me = lax.axis_index("ctx")
+    width = grads.shape[1] // group
+    if group > 4:
+        share = lax.psum_scatter(grads, "ctx", scatter_dimension=1, tiled=True)
+    else:
+        share = lax.dynamic_slice_in_dim(grads, me * width, width, 1)
+        for k in range(1, group):
+            block = lax.dynamic_slice_in_dim(grads, ((me + k) % group) * width, width, 1)
+            share = share + passed_along(block, "ctx", k)
+    return share + pair_swap(share, "seq", 1)
+
+
+def head_sum(partial):
+    half = partial.shape[0] // 2
+    core = lax.axis_index("head") % 2
+    mine = lax.dynamic_slice_in_dim(partial, core * half, half, 0)
+    theirs = lax.dynamic_slice_in_dim(partial, (1 - core) * half, half, 0).astype(jnp.bfloat16)
+    pair = (mine + pair_swap(theirs, "head", 1).astype(jnp.float32)).astype(jnp.bfloat16)
+    far = pair_swap(pair, "head", 2)
+    total = (pair.astype(jnp.float32) + far.astype(jnp.float32)).astype(jnp.bfloat16)
+    other = pair_swap(total, "head", 1)
+    first = core == 0
+    return jnp.concatenate(
+        [jnp.where(first, total, other), jnp.where(first, other, total)], axis=0
+    ).astype(jnp.float32)
+
+
+def swap_blocks(blocks, sign):
+    group = lax.axis_size("ctx")
+    me = lax.axis_index("ctx")
+    got = [lax.dynamic_index_in_dim(blocks, me, 0, keepdims=False)]
+    for k in range(1, group):
+        send = lax.dynamic_index_in_dim(blocks, (me + k) % group, 0, keepdims=False)
+        got.append(passed_along(send, "ctx", k))
+    stacked = jnp.stack(got)
+    return [
+        lax.dynamic_index_in_dim(stacked, (me - j) % group, 0, keepdims=False)
+        for j in range(group)
+    ]
+
+
+def turn(values, cosine, sine):
+    half = HD // 2
+    lower, upper = values[..., :half, :], values[..., half:, :]
+    return jnp.concatenate(
+        [lower * cosine - upper * sine, upper * cosine + lower * sine], axis=-2
+    )
+
+
+def tables(positions):
+    frequency = theta_base ** (-(jnp.arange(HD // 2, dtype=jnp.float32) * (2.0 / HD)))
+    angles = frequency[:, None] * positions.astype(jnp.float32)[None, :]
+    return (jnp.cos(angles), jnp.sin(angles))
+
+
+def attend(q, k, v, doc):
+    allowed = (doc[:, None] == doc[None, :])[None]
+    scores = jnp.einsum("ndi,ndj->nij", q, k, preferred_element_type=jnp.float32)
+    scores = jnp.where(allowed, scores, masked_score)
+    top = jnp.max(scores, axis=2)
+    weights = jnp.where(allowed, jnp.exp(scores - top[:, :, None]), 0.0)
+    total = jnp.sum(weights, axis=2)
+    out = jnp.einsum(
+        "ndj,nij->ndi", v, weights.astype(jnp.bfloat16), preferred_element_type=jnp.float32
+    )
+    return (out / total[:, None, :], top + jnp.log(total))
+
+
+def attend_back(q, k, v, doc, lse, out, grad):
+    allowed = (doc[:, None] == doc[None, :])[None]
+    delta = jnp.sum(grad.astype(jnp.float32) * out, axis=1)
+    scores = jnp.einsum("ndi,ndj->nij", q, k, preferred_element_type=jnp.float32)
+    probs = jnp.where(allowed, jnp.exp(scores - lse[:, :, None]), 0.0)
+    grad_v = jnp.einsum(
+        "ndi,nij->ndj", grad, probs.astype(jnp.bfloat16), preferred_element_type=jnp.float32
+    )
+    grad_probs = jnp.einsum("ndi,ndj->nij", grad, v, preferred_element_type=jnp.float32)
+    grad_s = (probs * (grad_probs - delta[:, :, None])).astype(jnp.bfloat16)
+    grad_q = jnp.einsum("ndj,nij->ndi", k, grad_s, preferred_element_type=jnp.float32)
+    grad_k = jnp.einsum("ndi,nij->ndj", q, grad_s, preferred_element_type=jnp.float32)
+    return (grad_q, grad_k, grad_v)
+
+
+def per_device(tokens, doc_lengths, norm_gains, w_qkv, w_out, w_in, w_down, cotangent):
+    rows = tokens.shape[1]
+    hidden = tokens[0].astype(jnp.float32)
+    lengths = doc_lengths[0]
+    group = lax.axis_size("ctx")
+    me = lax.axis_index("ctx")
+    width = w_qkv.shape[2]
+    heads = width // HD
+    each = heads // group
+    scale = HD ** (-0.5)
+    gains = gather_gains(norm_gains).astype(jnp.float32)
+    qkv_full = gather_weight(w_qkv, 1)
+    out_full = gather_weight(w_out, 1)
+    in_full = gather_weight(w_in, 1)
+    down_full = gather_weight(w_down, 1)
+    doc_all, pos_all = token_layout(lengths, jnp.int32(0), rows * group)
+    cos_all, sin_all = tables(pos_all)
+    cos_here = lax.dynamic_slice_in_dim(cos_all, me * rows, rows, 1)
+    sin_here = lax.dynamic_slice_in_dim(sin_all, me * rows, rows, 1)
+
+    normed_one, inverse_one, scaled_one = layer_norm(hidden, gains[0])
+    input_one = scaled_one.astype(jnp.bfloat16)
+    raw = jnp.einsum("cdn,td->cnt", qkv_full, input_one, preferred_element_type=jnp.float32)
+    raw = raw.reshape(3, heads, HD, rows)
+    q = (turn(raw[0], cos_here, sin_here) * scale).astype(jnp.bfloat16)
+    k = turn(raw[1], cos_here, sin_here).astype(jnp.bfloat16)
+    v = raw[2].astype(jnp.bfloat16)
+    blocks = jnp.stack([q, k, v], axis=1).reshape(group, each, 3, HD, rows)
+    mine = jnp.concatenate(swap_blocks(blocks, 1), axis=-1)
+    q, k, v = (mine[:, 0], mine[:, 1], mine[:, 2])
+    attn_float, lse = attend(q, k, v, doc_all)
+    parts = attn_float.astype(jnp.bfloat16).reshape(each, HD, group, rows).transpose(2, 0, 1, 3)
+    attn_low = jnp.concatenate(swap_blocks(parts, -1), axis=0).reshape(width, rows)
+
+    partial_out = jnp.einsum("nt,nd->td", attn_low, out_full, preferred_element_type=jnp.float32)
+    resid_one = hidden + head_sum(partial_out)
+    normed_two, inverse_two, scaled_two = layer_norm(resid_one, gains[1])
+    input_two = scaled_two.astype(jnp.bfloat16)
+    gate_up = jnp.einsum("td,cdf->tcf", input_two, in_full, preferred_element_type=jnp.float32)
+    activated, gelu_back = jax.vjp(exact_gelu, gate_up[:, 0])
+    mixed_low = (activated * gate_up[:, 1]).astype(jnp.bfloat16)
+    partial_ffn = jnp.dot(mixed_low, down_full, preferred_element_type=jnp.float32)
+
+    grad_rows = cotangent[0]
+    grad_mixed = jnp.einsum("td,fd->tf", grad_rows, down_full, preferred_element_type=jnp.float32)
+    grad_gate = gelu_back(grad_mixed * gate_up[:, 1])[0]
+    grad_up = grad_mixed * activated
+    grad_gate_up = jnp.stack([grad_gate, grad_up], axis=1).astype(jnp.bfloat16)
+    partial_two = jnp.einsum(
+        "tcf,cdf->td", grad_gate_up, in_full, preferred_element_type=jnp.float32
+    )
+    grad_input_two = head_sum(partial_two)
+    grad_down = jnp.einsum(
+        "tf,td->fd", mixed_low, grad_rows, preferred_element_type=jnp.float32
+    ).astype(jnp.bfloat16)
+    grad_in = jnp.einsum(
+        "td,tcf->cdf", input_two, grad_gate_up, preferred_element_type=jnp.float32
+    ).astype(jnp.bfloat16)
+    grad_input_two, grad_down, grad_in = lax.optimization_barrier(
+        (grad_input_two, grad_down, grad_in)
+    )
+    share_down = reduce_weight(grad_down)
+    share_in = reduce_weight(grad_in)
+    result = (resid_one + head_sum(partial_ffn)).astype(jnp.bfloat16)
+    grad_norm_two, gain_grad_two = norm_back(grad_input_two, normed_two, inverse_two, gains[1])
+    grad_resid = grad_rows.astype(jnp.float32) + grad_norm_two
+    grad_branch = grad_resid.astype(jnp.bfloat16)
+    grad_attn = jnp.einsum(
+        "nd,td->nt", out_full, grad_branch, preferred_element_type=jnp.float32
+    ).astype(jnp.bfloat16)
+    grad_mine = jnp.concatenate(
+        swap_blocks(grad_attn.reshape(group, each, HD, rows), 1), axis=-1
+    )
+    grad_out = jnp.einsum(
+        "nt,td->nd", attn_low, grad_branch, preferred_element_type=jnp.float32
+    ).astype(jnp.bfloat16)
+    grad_mine, grad_out = lax.optimization_barrier((grad_mine, grad_out))
+    share_out = reduce_weight(grad_out)
+    grad_q, grad_k, grad_v = attend_back(q, k, v, doc_all, lse, attn_float, grad_mine)
+    grad_q = turn(grad_q, cos_all, -sin_all) * scale
+    grad_k = turn(grad_k, cos_all, -sin_all)
+    back = jnp.stack([grad_q, grad_k, grad_v], axis=1).astype(jnp.bfloat16)
+    back = back.reshape(each, 3, HD, group, rows).transpose(3, 0, 1, 2, 4)
+    grad_raw = jnp.concatenate(swap_blocks(back, -1), axis=0)
+    grad_raw = grad_raw.transpose(1, 0, 2, 3).reshape(3, width, rows)
+    partial_one = jnp.einsum(
+        "cnt,cdn->td", grad_raw, qkv_full, preferred_element_type=jnp.float32
+    )
+    grad_qkv = jnp.einsum(
+        "td,cnt->cdn", input_one, grad_raw, preferred_element_type=jnp.float32
+    ).astype(jnp.bfloat16)
+    partial_one, grad_qkv, share_down, share_in, share_out = lax.optimization_barrier(
+        (partial_one, grad_qkv, share_down, share_in, share_out)
+    )
+    share_qkv = reduce_weight(grad_qkv)
+    grad_input_one = head_sum(partial_one)
+    grad_norm_one, gain_grad_one = norm_back(grad_input_one, normed_one, inverse_one, gains[0])
+    grad_tokens = (grad_resid + grad_norm_one).astype(jnp.bfloat16)
+    total_gains = reduce_gains(jnp.stack([gain_grad_one, gain_grad_two]))
+    return (
+        result[None],
+        grad_tokens[None],
+        total_gains,
+        reduce_weight_rows(share_qkv),
+        reduce_weight_rows(share_out),
+        reduce_weight_rows(share_in),
+        reduce_weight_rows(share_down),
+    )
+
+
 def solution(mesh):
+    heads = 1024 // HD // mesh.shape["head"]
+    body = per_device if heads % mesh.shape["ctx"] == 0 else per_device_ring
     return jax.shard_map(
-        per_device,
+        body,
         mesh=mesh,
         in_specs=(
             P("seq", "ctx", None),

time: 748 us -> 619 us (0.83)
  waiting for transfers between devices: 476 us -> 225 us
  local copies, waits for them, and re-layouts: 18.5 us -> 117 us
  other arithmetic: 66.9 us -> 92.9 us
  starting transfers between devices: 16.1 us -> 37 us
  matrix products: 107 us -> 96.5 us
  blocking collectives: 38.1 us -> 28.2 us
    psum x4 -> x0, waiting for transfers between devices: 148 us -> none  [the longest x1 45.3 us: per_device(): lax.psum(share_qkv.astype(jnp.bfloat16), 'seq').astype(jnp.float32)]
    reduce_scatter x4 -> x0, waiting for transfers between devices: 145 us -> none  [the longest x1 54.3 us: per_device(): lax.psum_scatter(grad_in.astype(jnp.bfloat16), 'ctx', scatter_dimension=1...]
    all_gather x5 -> x3, waiting for transfers between devices: 117 us -> 39.2 us  [gather_weight(): return lax.all_gather(mine, ('ctx', 'seq'), axis=dim, tiled=True)]
    unnamed x15 -> x11, waiting for transfers between devices: 19.4 us -> 86.3 us
    ppermute x0 -> x17, waiting for transfers between devices: none -> 46.6 us  [pair_swap(): return lax.ppermute(block, axis, [(i, i ^ mask) for i in range(size)])]
    unnamed x90 -> x85, local copies, waits for them, and re-layouts: 10.5 us -> 47.6 us
    dot_general x0 -> x1, local copies, waits for them, and re-layouts: none -> 27.3 us  [attend(): jnp.einsum('ndi,ndj->nij', q, k, preferred_element_type=jnp.float32)]
    exp x0 -> x1, local copies, waits for them, and re-layouts: none -> 27.3 us  [attend_back(): probs = jnp.where(allowed, jnp.exp(scores - lse[:, :, None]), 0.0)]
  transfers between devices with their start and end apart: 28 -> 42, of which waited for: 22 -> 20; matrix products, arithmetic and copies ran while one was open for 20% -> 42% of each run, Pallas kernels for 0% -> 0%
where the time goes in v1:
time: 619 us; the launch traced here: 612 us
  waiting for transfers between devices  225 us (36%)
  local copies, waits for them, and re-layouts  117 us (19%)
  matrix products  96.5 us (16%)
  other arithmetic  92.9 us (15%)
  starting transfers between devices  37 us (6%)
  blocking collectives  28.2 us (5%)
  between operations  15.6 us (3%)
    unnamed x11, waiting for transfers between devices  86.3 us
    ppermute x18, waiting for transfers between devices, passed_along(): return lax.ppermute(block, axis, route)  53.3 us
    unnamed x85, local copies, waits for them, and re-layouts  47.6 us
    ppermute x17, waiting for transfers between devices, pair_swap(): return lax.ppermute(block, axis, [(i, i ^ mask) for i in range(size)])  46.6 us
    all_gather x3, waiting for transfers between devices, gather_weight(): return lax.all_gather(mine, ('ctx', 'seq'), axis=dim, tiled=True)  39.2 us
    all_gather x1, blocking collectives, gather_weight(): return lax.all_gather(mine, ('ctx', 'seq'), axis=dim, tiled=True)  28.2 us
    dot_general x1, local copies, waits for them, and re-layouts, attend(): jnp.einsum('ndi,ndj->nij', q, k, preferred_element_type=jnp.float32)  27.3 us
    exp x1, local copies, waits for them, and re-layouts, attend_back(): probs = jnp.where(allowed, jnp.exp(scores - lse[:, :, None]), 0.0)  27.3 us
  transfers between devices with their start and end apart: 42, of which 20 were waited for; matrix products, arithmetic and copies ran while one was open for 42% of the time, Pallas kernels for 0%

profile of v1, /device:TPU:0, one launch (start us, length us, event | category | flops | bytes accessed | tf_op | source)
XLA Modules:
  0.0 612.3 jit_solution(3698907161401412753)
XLA Ops:
  9.2 3.1 collective-permute-start
  12.3 2.1 collective-permute-start.2
  15.3 1.6 constant_dynamic-slice_fusion.8
  19.5 39.2 %all-gather.4.cloned.1.call-done = bf16[3,1024,256]{1,2,0:T(8,128)(2,1)} async-done(((bf16[3,128,256]{1,2,0:T(8,128)(2,1)}), bf16[3,1024,256]{1,2,0:T(8,128)(2,1)}) %all-gather.4.cloned.1.call-update) | async-done | bytes 1572880 | tf_op jit(solution)/shard_map/all_gather | solution.py:289
  58.7 3.0 fusion.74
  63.0 3.8 collective-permute-start.5
  67.9 7.8 %collective-permute-done.3 = bf16[1,3,64,640]{3,2,1,0:T(8,128)(2,1)S(1)} collective-permute-done((bf16[1,3,64,640]{3,2,1,0:T(8,128)(2,1)}, bf16[1,3,64,640]{3,2,1,0:T(8,128)(2,1)S(1)}, u32[]{:S(2)}, u32[]{:S(2)}) %collective-permute-start.3) | collective-permute-done | bytes 245792 | tf_op jit(solution)/shard_map/ppermute | solution.py:17
  75.7 3.2 collective-permute-done.5
  78.9 13.9 %collective-permute-done.4 = bf16[1,3,64,640]{3,2,1,0:T(8,128)(2,1)} collective-permute-done((bf16[1,3,64,640]{3,2,1,0:T(8,128)(2,1)S(1)}, bf16[1,3,64,640]{3,2,1,0:T(8,128)(2,1)}, u32[]{:S(2)}, u32[]{:S(2)}) %collective-permute-start.4) | collective-permute-done | bytes 245792 | tf_op jit(solution)/shard_map/ppermute | solution.py:17
  94.1 10.7 %fusion.115 = f32[2560,2560]{0,1:T(8,128)} fusion(bf16[1,3,64,2560]{3,2,1,0:T(8,128)(2,1)S(1)} %pad_maximum_fusion.7), kind=kOutput, calls=%fused_computation.210 | convolution fusion | flops 838860800 | bytes 26869760 | tf_op jit(solution)/shard_map/ndi,ndj->nij/dot_general | solution.py:376
  104.8 27.3 %copy.64 = f32[2560,2560]{1,0:T(8,128)} copy(f32[2560,2560]{0,1:T(8,128)} %fusion.115) | data formatting | bytes 52428800 | tf_op jit(solution)/shard_map/ndi,ndj->nij/dot_general | solution.py:376
  132.1 9.6 %fusion.3 = f32[2560]{0:T(1024)S(1)} fusion(f32[2560,2560]{1,0:T(8,128)} %copy.64, s32[2560]{0:T(1024)S(1)} %get-tuple-element.61), kind=kLoop, calls=%fused_computation.8 | loop fusion | flops 19658240 | bytes 26234880 | tf_op jit(solution)/shard_map/reduce_max | solution.py:378
  141.7 6.8 %copy-done.3 = f32[2560,2560]{1,0:T(8,128)S(1)} copy-done((f32[2560,2560]{1,0:T(8,128)S(1)}, f32[2560,2560]{1,0:T(8,128)}, u32[]{:S(2)}) %copy-start.3) | copy-done | bytes 26214424
  148.5 7.6 %fusion.4 = f32[2560]{0:T(1024)S(1)} fusion(f32[2560,2560]{1,0:T(8,128)S(1)} %copy-done.3, f32[2560]{0:T(1024)S(1)} %fusion.3, s32[2560]{0:T(1024)S(1)} %get-tuple-element.61), kind=kLoop, calls=%fused_computation.9 | loop fusion | flops 32765440 | bytes 26245120 | tf_op jit(solution)/shard_map/reduce_sum | solution.py:380
  156.1 12.3 %fusion.166 = (bf16[64,2560]{1,0:T(8,128)(2,1)S(1)}, f32[64,2560]{1,0:T(8,128)}) fusion(f32[2560]{0:T(1024)S(1)} %fusion.4, f32[2560,2560]{1,0:T(8,128)} %copy.64, f32[2560]{0:T(1024)S(1)} %fusion.3, s32[2560]{0:T(1024)S(1)} %get-tuple-element.61, bf16[1,3,64,2560]{3,2,1,0:T(8,128)(2,1)S(1)} %pad_maximum_fusion.7), kind=kOutput, calls=%fused_computation.333 | convolution fusion | flops 871956480 | bytes 27574272 | tf_op jit(solution)/shard_map/ndj,nij->ndi/dot_general | solution.py:381
  171.3 28.2 %all_gather.13 = bf16[256,1024]{1,0:T(8,128)(2,1)S(1)} all-gather(bf16[256,128]{1,0:T(8,128)(2,1)S(1)} %constant_dynamic-slice_fusion.10), channel_id=1, replica_groups=mesh['seq'=2,'ctx'=4,'head'=4] {'ctx','seq'}, dimensions={1}, use_global_device_ids=true | all-gather | bytes 589824 | tf_op jit(solution)/shard_map/all_gather | solution.py:289
  202.1 2.1 collective-permute-done.9
  205.7 1.7 collective-permute-start.10
  207.4 15.1 %collective-permute-done.10 = bf16[320,1024]{1,0:T(8,128)(2,1)S(1)} collective-permute-done((bf16[320,1024]{1,0:T(8,128)(2,1)S(1)}, bf16[320,1024]{1,0:T(8,128)(2,1)S(1)}, u32[]{:S(2)}, u32[]{:S(2)}) %collective-permute-start.10) | collective-permute-done | bytes 655392 | tf_op jit(solution)/shard_map/ppermute | solution.py:283
  222.9 4.3 fusion.77
  229.6 4.4 fusion.117
  234.0 4.3 fusion.91
  240.7 2.3 convolution_bitcast_fusion.3
  243.5 1.8 collective-permute-done.15
  245.5 1.7 collective-permute-start.16
  247.2 15.3 %collective-permute-done.16 = bf16[320,1024]{1,0:T(8,128)(2,1)S(1)} collective-permute-done((bf16[320,1024]{1,0:T(8,128)(2,1)S(1)}, bf16[320,1024]{1,0:T(8,128)(2,1)S(1)}, u32[]{:S(2)}, u32[]{:S(2)}) %collective-permute-start.16) | collective-permute-done | bytes 655392 | tf_op jit(solution)/shard_map/ppermute | solution.py:283
  262.9 5.4 convolution_convert_fusion.1
  268.3 4.0 convert_bitcast_fusion.1
  272.7 1.9 multiply_reduce_fusion
  274.7 13.9 %multiply_add_fusion = f32[640,1024]{1,0:T(8,128)S(1)} fusion(f32[640,1024]{1,0:T(8,128)S(1)} %maximum_convert_fusion, bf16[1,640,1024]{2,1,0:T(8,128)(2,1)S(1)} %copy-done.16, f32[640]{0:T(1024)S(1)} %get-tuple-element.137, f32[640]{0:T(1024)S(1)} %get-tuple-element.138, f32[1024]{0:T(1024)S(1)} %bitcast.416, f32[640]{0:T(1024)S(1)} %add_rsqrt_fusion, ...), kind=kLoop, calls=%fused_computation.45 | loop fusion | flops 9830400 | bytes 9189376 | tf_op jit(solution)/shard_map/add | solution.py:467
  292.0 3.3 collective-permute-start.20
  295.4 3.3 collective-permute-done.18
  298.7 3.0 collective-permute-done.19
  301.8 2.0 copy.84
  303.9 2.6 copy.80
  306.5 22.7 %fusion.2 = (bf16[2560,2560]{1,0:T(8,128)(2,1)}, f32[2560,2560]{0,1:T(8,128)}) fusion(s32[2560]{0:T(1024)S(1)} %get-tuple-element.61, f32[2560,2560]{0,1:T(8,128)} %fusion.115, f32[2560]{0:T(1024)S(1)} %log_add_fusion), kind=kLoop, calls=%fused_computation.6 | loop fusion | flops 19660800 | bytes 65556480 | tf_op jit(solution)/shard_map/convert_element_type | solution.py:393
  329.2 27.3 %copy.69 = f32[2560,2560]{1,0:T(8,128)} copy(f32[2560,2560]{0,1:T(8,128)} %get-tuple-element.64) | data formatting | bytes 52428800 | tf_op jit(solution)/shard_map/exp | solution.py:391
  356.5 4.1 fusion.86
  363.1 8.7 %copy.82 = bf16[2,1024,656]{2,0,1:T(2,128)(2,1)} copy(bf16[2,1024,656]{1,2,0:T(8,128)(2,1)} %convert_bitcast_fusion.1) | data formatting | bytes 5373952
  371.8 7.5 %reshape.611 = bf16[1024,1312]{1,0:T(8,128)(2,1)} reshape(bf16[1024,2,656]{2,1,0:T(2,128)(2,1)} %bitcast.376) | data formatting | bytes 5373952
  380.6 14.4 %fusion.1 = bf16[2560,2560]{1,0:T(8,128)(2,1)} fusion(f32[2560,2560]{1,0:T(8,128)} %copy.69, f32[2560]{0:T(1024)S(1)} %fusion.94, s32[2560]{0:T(1024)S(1)} %get-tuple-element.61, bf16[1,64,2560]{2,1,0:T(8,128)(2,1)S(1)} %pad_maximum_fusion.13, bf16[1,3,64,2560]{3,2,1,0:T(8,128)(2,1)} %copy-done.8), kind=kOutput, calls=%fused_computation.4 | convolution fusion | flops 871628800 | bytes 40013824 | tf_op jit(solution)/shard_map/ndi,ndj->nij/dot_general | solution.py:395
  395.0 8.3 %convolution_bitcast_fusion = f32[1,64,2560]{2,1,0:T(8,128)} fusion(bf16[2560,2560]{1,0:T(8,128)(2,1)} %fusion.1, bf16[1,3,64,2560]{3,2,1,0:T(8,128)(2,1)} %copy-done.8), kind=kOutput, calls=%fused_computation.16 | convolution fusion | flops 838860800 | bytes 14090240 | tf_op jit(solution)/shard_map/ndi,nij->ndj/dot_general | solution.py:398
  403.9 5.9 convolution_bitcast_fusion.1
  409.8 2.6 fusion.101
  414.0 9.5 %fusion.85 = bf16[1,1,64,4,640]{4,2,3,1,0:T(8,128)(2,1)} fusion(bf16[4,640,2560]{2,1,0:T(8,128)(2,1)} %bitcast.373, bf16[1,64,2560]{2,1,0:T(8,128)(2,1)S(1)} %pad_maximum_fusion.13), kind=kOutput, calls=%fused_computation.143 | convolution fusion | flops 839024640 | bytes 13762560 | tf_op jit(solution)/shard_map/ndi,nij->ndj/dot_general | solution.py:392
  425.1 2.3 collective-permute-start.23
  428.1 2.2 add_convert_fusion.5
  430.3 1.6 collective-permute-start.13
  431.9 3.2 collective-permute-done.23
  435.1 16.7 %collective-permute-done.22 = bf16[1,3,64,640]{3,2,1,0:T(8,128)(2,1)S(1)} collective-permute-done((bf16[1,3,64,640]{3,2,1,0:T(8,128)(2,1)S(1)}, bf16[1,3,64,640]{3,2,1,0:T(8,128)(2,1)S(1)}, u32[]{:S(2)}, u32[]{:S(2)}) %collective-permute-start.22) | collective-permute-done | bytes 245792 | tf_op jit(solution)/shard_map/ppermute | solution.py:17
  453.7 2.7 convolution_bitcast_fusion.2
  456.4 2.8 fusion.68
  461.8 55.8 %reduce-scatter.15.cloned.1.call-done = bf16[128,1312]{1,0:T(8,128)(2,1)} async-done(((bf16[1024,1312]{1,0:T(8,128)(2,1)}), bf16[128,1312]{1,0:T(8,128)(2,1)}) %reduce-scatter.15.cloned.1.call-update) | async-done | bytes 335888
  519.9 2.3 dynamic-slice_convert_fusion
  522.1 2.4 add_convert_fusion.4
  525.0 4.1 copy.86
  529.2 3.1 copy.97
  532.3 1.7 add_convert_fusion.1
  538.3 2.0 fusion.29
  543.1 7.7 %collective-permute-done.25 = bf16[320,1024]{1,0:T(8,128)(2,1)S(1)} collective-permute-done((bf16[320,1024]{1,0:T(8,128)(2,1)S(1)}, bf16[320,1024]{1,0:T(8,128)(2,1)S(1)}, u32[]{:S(2)}, u32[]{:S(2)}) %collective-permute-start.25) | collective-permute-done | bytes 655392 | tf_op jit(solution)/shard_map/ppermute | solution.py:283
  552.1 4.2 collective-permute-done.33
  560.1 2.2 collective-permute-start.28
  566.5 30.4 %reduce-scatter.19.cloned.1.call-done = bf16[128,768]{1,0:T(8,128)(2,1)} async-done(((bf16[1024,768]{1,0:T(8,128)(2,1)}), bf16[128,768]{1,0:T(8,128)(2,1)}) %reduce-scatter.19.cloned.1.call-update) | async-done | bytes 196624
  599.3 3.7 fusion.72
  (235 shorter events, 62.1 us)
Async XLA Ops:
  7.2 59.6 %copy-start = (bf16[2,256,656]{1,2,0:T(8,128)(2,1)S(1)}, bf16[2,256,656]{1,2,0:T(8,128)(2,1)}, u32[]{:S(2)}) copy-start(bf16[2,256,656]{1,2,0:T(8,128)(2,1)} %param.13) | copy-start | bytes 2015236
  7.2 10.7 %copy-start.4 = (bf16[1,640,1024]{2,1,0:T(8,128)(2,1)S(1)}, bf16[1,640,1024]{2,1,0:T(8,128)(2,1)}, u32[]{:S(2)}) copy-start(bf16[1,640,1024]{2,1,0:T(8,128)(2,1)} %param.8) | copy-start | bytes 3932164
  7.2 51.5 %all-gather.4.cloned.1.call-start = ((), (), s32[]{:S(2)}) async-start(), calls=%async_computation.4 | async-start | bytes 1769472 | tf_op jit(solution)/shard_map/all_gather | solution.py:289
  9.1 9.5 %copy-start.32 = (s32[1,4]{1,0:T(1,128)S(1)}, s32[1,4]{1,0:T(1,128)}, u32[]{:S(2)}) copy-start(s32[1,4]{1,0:T(1,128)} %param.9) | copy-start | bytes 52
  9.2 213.7 %all-gather.8.cloned.1.call-start = ((), (), s32[]{:S(2)}) async-start(), calls=%async_computation.6 | async-start | bytes 1511424 | tf_op jit(solution)/shard_map/all_gather | solution.py:289
  9.2 10.2 %collective-permute-start = (bf16[2,256]{1,0:T(2,128)(2,1)}, bf16[2,256]{1,0:T(2,128)(2,1)S(1)}, u32[]{:S(2)}, u32[]{:S(2)}) collective-permute-start(bf16[2,256]{1,0:T(2,128)(2,1)} %param.10), channel_id=1, source_target_pairs={{12,0},{0,4},{4,8},{8,12},{13,1},{1,5},{5,9},{9,13},{14,2},{2,6},{... | collective-permute-start | bytes 3080 | tf_op jit(solution)/shard_map/ppermute | solution.py:17
  12.3 7.2 %collective-permute-start.2 = (bf16[2,256]{1,0:T(2,128)(2,1)}, bf16[2,256]{1,0:T(2,128)(2,1)S(1)}, u32[]{:S(2)}, u32[]{:S(2)}) collective-permute-start(bf16[2,256]{1,0:T(2,128)(2,1)} %param.10), channel_id=1, source_target_pairs={{4,0},{8,4},{12,8},{0,12},{5,1},{9,5},{13,9},{1,13},{6,2},{10,6},{... | collective-permute-start | bytes 3080 | tf_op jit(solution)/shard_map/ppermute | solution.py:17
  14.4 5.0 collective-permute-start.1
  17.0 212.6 %all-gather.6.cloned.1.call-start = ((), (), s32[]{:S(2)}) async-start(), calls=%async_computation.5 | async-start | bytes 3022848 | tf_op jit(solution)/shard_map/all_gather | solution.py:289
  18.1 43.5 %copy-start.21 = (f32[640]{0:T(1024)}, f32[640]{0:T(1024)S(1)}, u32[]{:S(2)}) copy-start(f32[640]{0:T(1024)S(1)} %broadcast_multiply_fusion.6) | copy-start | bytes 7684
  18.8 42.9 %copy-start.19 = (f32[2560]{0:T(1024)}, f32[2560]{0:T(1024)S(1)}, u32[]{:S(2)}) copy-start(f32[2560]{0:T(1024)S(1)} %subtract_convert_fusion.1) | copy-start | bytes 30724
  19.3 42.3 %copy-start.24 = (f32[640]{0:T(1024)}, f32[640]{0:T(1024)S(1)}, u32[]{:S(2)}) copy-start(f32[640]{0:T(1024)S(1)} %add_rsqrt_fusion.1) | copy-start | bytes 7684
  19.5 42.2 %copy-start.26 = (f32[1,1024]{1,0:T(1,128)}, f32[1,1024]{1,0:T(1,128)S(1)}, u32[]{:S(2)}) copy-start(f32[1,1024]{1,0:T(1,128)S(1)} %get-tuple-element.134) | copy-start | bytes 12292
  62.2 5.7 copy-start.28
  63.0 12.7 %collective-permute-start.3 = (bf16[1,3,64,640]{3,2,1,0:T(8,128)(2,1)}, bf16[1,3,64,640]{3,2,1,0:T(8,128)(2,1)S(1)}, u32[]{:S(2)}, u32[]{:S(2)}) collective-permute-start(bf16[1,3,64,640]{3,2,1,0:T(8,128)(2,1)} %get-tuple-element.90), channel_id=1, source_target_pairs={{12,0},{0,4},{4,8},{8,12},{13,1},{1,5},{5,9},{9,13},{14,2},{2,6},{... | collective-permute-start | bytes 737288 | tf_op jit(solution)/shard_map/ppermute | solution.py:17
  63.0 15.9 %collective-permute-start.5 = (bf16[1,3,64,640]{3,2,0,1:T(8,128)(2,1)S(1)}, bf16[1,3,64,640]{3,2,0,1:T(8,128)(2,1)S(1)}, u32[]{:S(2)}, u32[]{:S(2)}) collective-permute-start(bf16[1,3,64,640]{3,2,0,1:T(8,128)(2,1)S(1)} %get-tuple-element.91), channel_id=1, source_target_pairs={{4,0},{8,4},{12,8},{0,12},{5,1},{9,5},{13,9},{1,13},{6,2},{10,6},{... | collective-permute-start | bytes 737288 | tf_op jit(solution)/shard_map/ppermute | solution.py:17
  66.8 26.0 %collective-permute-start.4 = (bf16[1,3,64,640]{3,2,1,0:T(8,128)(2,1)S(1)}, bf16[1,3,64,640]{3,2,1,0:T(8,128)(2,1)}, u32[]{:S(2)}, u32[]{:S(2)}) collective-permute-start(bf16[1,3,64,640]{3,2,1,0:T(8,128)(2,1)S(1)} %get-tuple-element.92), channel_id=1, source_target_pairs={{8,0},{12,4},{0,8},{4,12},{9,1},{13,5},{1,9},{5,13},{10,2},{14,6},... | collective-permute-start | bytes 737288 | tf_op jit(solution)/shard_map/ppermute | solution.py:17
  67.6 391.6 %reduce-scatter.17.cloned.1.call-start = ((), (), s32[]{:S(2)}) async-start(), calls=%async_computation.9 | async-start | bytes 589824
  94.1 62.0 %copy-start.8 = (bf16[1,3,64,2560]{3,2,1,0:T(8,128)(2,1)}, bf16[1,3,64,2560]{3,2,1,0:T(8,128)(2,1)S(1)}, u32[]{:S(2)}) copy-start(bf16[1,3,64,2560]{3,2,1,0:T(8,128)(2,1)S(1)} %pad_maximum_fusion.7) | copy-start | bytes 2949124
  132.1 16.4 %copy-start.3 = (f32[2560,2560]{1,0:T(8,128)S(1)}, f32[2560,2560]{1,0:T(8,128)}, u32[]{:S(2)}) copy-start(f32[2560,2560]{1,0:T(8,128)} %copy.64) | copy-start | bytes 78643200
  169.2 30.4 %collective-permute-start.8 = (bf16[1,64,640]{2,1,0:T(8,128)(2,1)S(1)}, bf16[1,64,640]{2,1,0:T(8,128)(2,1)S(1)}, u32[]{:S(2)}, u32[]{:S(2)}) collective-permute-start(bf16[1,64,640]{2,1,0:T(8,128)(2,1)S(1)} %bitcast.411), channel_id=1, source_target_pairs={{4,0},{8,4},{12,8},{0,12},{5,1},{9,5},{13,9},{1,13},{6,2},{10,6},{... | collective-permute-start | bytes 245768 | tf_op jit(solution)/shard_map/ppermute | solution.py:17
  170.6 29.0 %collective-permute-start.6 = (bf16[1,64,640]{2,1,0:T(8,128)(2,1)S(1)}, bf16[1,64,640]{2,1,0:T(8,128)(2,1)S(1)}, u32[]{:S(2)}, u32[]{:S(2)}) collective-permute-start(bf16[1,64,640]{2,1,0:T(8,128)(2,1)S(1)} %bitcast.410), channel_id=1, source_target_pairs={{12,0},{0,4},{4,8},{8,12},{13,1},{1,5},{5,9},{9,13},{14,2},{2,6},{... | collective-permute-start | bytes 245768 | tf_op jit(solution)/shard_map/ppermute | solution.py:17
  171.3 28.3 %collective-permute-start.7 = (bf16[1,64,640]{2,1,0:T(8,128)(2,1)S(1)}, bf16[1,64,640]{2,1,0:T(8,128)(2,1)S(1)}, u32[]{:S(2)}, u32[]{:S(2)}) collective-permute-start(bf16[1,64,640]{2,1,0:T(8,128)(2,1)S(1)} %bitcast.409), channel_id=1, source_target_pairs={{8,0},{12,4},{0,8},{4,12},{9,1},{13,5},{1,9},{5,13},{10,2},{14,6},... | collective-permute-start | bytes 245768 | tf_op jit(solution)/shard_map/ppermute | solution.py:17
  202.0 2.2 collective-permute-start.9
  205.7 16.8 %collective-permute-start.10 = (bf16[320,1024]{1,0:T(8,128)(2,1)S(1)}, bf16[320,1024]{1,0:T(8,128)(2,1)S(1)}, u32[]{:S(2)}, u32[]{:S(2)}) collective-permute-start(bf16[320,1024]{1,0:T(8,128)(2,1)S(1)} %add_convert_fusion.7), channel_id=1, source_target_pairs={{0,2},{1,3},{2,0},{3,1},{4,6},{5,7},{6,4},{7,5},{8,10},{9,11},{10,... | collective-permute-start | bytes 1966088 | tf_op jit(solution)/shard_map/ppermute | solution.py:283
  222.7 4.4 copy-start.15
  222.7 4.4 collective-permute-start.11
  229.6 4.4 copy-start.12
  234.0 28.9 %copy-start.7 = (f32[640,2,656]{0,2,1:T(8,128)}, f32[640,2,656]{0,2,1:T(8,128)S(1)}, u32[]{:S(2)}) copy-start(f32[640,2,656]{0,2,1:T(8,128)S(1)} %fusion.117) | copy-start | bytes 10076164
  243.1 19.8 %copy-start.16 = (bf16[1,640,1024]{2,1,0:T(8,128)(2,1)S(1)}, bf16[1,640,1024]{2,1,0:T(8,128)(2,1)}, u32[]{:S(2)}) copy-start(bf16[1,640,1024]{2,1,0:T(8,128)(2,1)} %param.15) | copy-start | bytes 3932164
  243.1 2.2 collective-permute-start.15
  245.5 17.0 %collective-permute-start.16 = (bf16[320,1024]{1,0:T(8,128)(2,1)S(1)}, bf16[320,1024]{1,0:T(8,128)(2,1)S(1)}, u32[]{:S(2)}, u32[]{:S(2)}) collective-permute-start(bf16[320,1024]{1,0:T(8,128)(2,1)S(1)} %add_convert_fusion.3), channel_id=1, source_target_pairs={{0,2},{1,3},{2,0},{3,1},{4,6},{5,7},{6,4},{7,5},{8,10},{9,11},{10,... | collective-permute-start | bytes 1966088 | tf_op jit(solution)/shard_map/ppermute | solution.py:283
  262.8 9.5 %collective-permute-start.17 = (bf16[320,1024]{1,0:T(8,128)(2,1)S(1)}, bf16[320,1024]{1,0:T(8,128)(2,1)S(1)}, u32[]{:S(2)}, u32[]{:S(2)}) collective-permute-start(bf16[320,1024]{1,0:T(8,128)(2,1)S(1)} %add_convert_fusion.2), channel_id=1, source_target_pairs={{0,1},{1,0},{2,3},{3,2},{4,5},{5,4},{6,7},{7,6},{8,9},{9,8},{10,11... | collective-permute-start | bytes 1966088 | tf_op jit(solution)/shard_map/ppermute | solution.py:283
  274.7 13.9 %copy-start.14 = (bf16[256,1024]{1,0:T(8,128)(2,1)S(1)}, bf16[256,1024]{1,0:T(8,128)(2,1)}, u32[]{:S(2)}) copy-start(bf16[256,1024]{1,0:T(8,128)(2,1)} %copy-done.13) | copy-start | bytes 1572868
  291.5 7.2 %collective-permute-start.18 = (bf16[1,64,640]{2,1,0:T(8,128)(2,1)S(1)}, bf16[1,64,640]{2,1,0:T(8,128)(2,1)S(1)}, u32[]{:S(2)}, u32[]{:S(2)}) collective-permute-start(bf16[1,64,640]{2,1,0:T(8,128)(2,1)S(1)} %get-tuple-element.111), channel_id=1, source_target_pairs={{12,0},{0,4},{4,8},{8,12},{13,1},{1,5},{5,9},{9,13},{14,2},{2,6},{... | collective-permute-start | bytes 245768 | tf_op jit(solution)/shard_map/ppermute | solution.py:17
  292.0 9.7 %collective-permute-start.19 = (bf16[1,64,640]{2,1,0:T(8,128)(2,1)S(1)}, bf16[1,64,640]{2,1,0:T(8,128)(2,1)S(1)}, u32[]{:S(2)}, u32[]{:S(2)}) collective-permute-start(bf16[1,64,640]{2,1,0:T(8,128)(2,1)S(1)} %get-tuple-element.112), channel_id=1, source_target_pairs={{8,0},{12,4},{0,8},{4,12},{9,1},{13,5},{1,9},{5,13},{10,2},{14,6},... | collective-permute-start | bytes 245768 | tf_op jit(solution)/shard_map/ppermute | solution.py:17
  292.0 9.6 %collective-permute-start.20 = (bf16[1,64,640]{2,1,0:T(8,128)(2,1)S(1)}, bf16[1,64,640]{2,1,0:T(8,128)(2,1)S(1)}, u32[]{:S(2)}, u32[]{:S(2)}) collective-permute-start(bf16[1,64,640]{2,1,0:T(8,128)(2,1)S(1)} %get-tuple-element.113), channel_id=1, source_target_pairs={{4,0},{8,4},{12,8},{0,12},{5,1},{9,5},{13,9},{1,13},{6,2},{10,6},{... | collective-permute-start | bytes 245768 | tf_op jit(solution)/shard_map/ppermute | solution.py:17
  303.8 156.9 %reduce-scatter.13.cloned.1.call-start = ((), (), s32[]{:S(2)}) async-start(), calls=%async_computation.7 | async-start | bytes 1769472
  306.5 211.1 %reduce-scatter.15.cloned.1.call-start = ((), (), s32[]{:S(2)}) async-start(), calls=%async_computation.8 | async-start | bytes 3244032
  363.1 65.0 %collective-permute-start.12 = (bf16[320,1024]{1,0:T(8,128)(2,1)}, bf16[320,1024]{1,0:T(8,128)(2,1)}, u32[]{:S(2)}, u32[]{:S(2)}) collective-permute-start(bf16[320,1024]{1,0:T(8,128)(2,1)} %dynamic-slice_convert_fusion.2), channel_id=1, source_target_pairs={{0,1},{1,0},{2,3},{3,2},{4,5},{5,4},{6,7},{7,6},{8,9},{9,8},{10,11... | collective-permute-start | bytes 1966088 | tf_op jit(solution)/shard_map/ppermute | solution.py:283
  379.3 217.6 %reduce-scatter.19.cloned.1.call-start = ((), (), s32[]{:S(2)}) async-start(), calls=%async_computation.10 | async-start | bytes 1769472
  395.0 9.0 %copy-start.2 = (bf16[2560,2560]{1,0:T(8,128)(2,1)S(1)}, bf16[2560,2560]{1,0:T(8,128)(2,1)}, u32[]{:S(2)}) copy-start(bf16[2560,2560]{1,0:T(8,128)(2,1)} %fusion.1) | copy-start | bytes 39321604
  403.9 5.9 copy-start.20
  403.9 5.9 copy-start.30
  424.8 3.3 copy-start.10
  425.1 10.1 %collective-permute-start.23 = (bf16[1,3,64,640]{3,2,1,0:T(8,128)(2,1)S(1)}, bf16[1,3,64,640]{3,2,1,0:T(8,128)(2,1)S(1)}, u32[]{:S(2)}, u32[]{:S(2)}) collective-permute-start(bf16[1,3,64,640]{3,2,1,0:T(8,128)(2,1)S(1)} %get-tuple-element.82), channel_id=1, source_target_pairs={{4,0},{8,4},{12,8},{0,12},{5,1},{9,5},{13,9},{1,13},{6,2},{10,6},{... | collective-permute-start | bytes 737288 | tf_op jit(solution)/shard_map/ppermute | solution.py:17
  427.3 24.5 %collective-permute-start.22 = (bf16[1,3,64,640]{3,2,1,0:T(8,128)(2,1)S(1)}, bf16[1,3,64,640]{3,2,1,0:T(8,128)(2,1)S(1)}, u32[]{:S(2)}, u32[]{:S(2)}) collective-permute-start(bf16[1,3,64,640]{3,2,1,0:T(8,128)(2,1)S(1)} %get-tuple-element.83), channel_id=1, source_target_pairs={{8,0},{12,4},{0,8},{4,12},{9,1},{13,5},{1,9},{5,13},{10,2},{14,6},... | collective-permute-start | bytes 737288 | tf_op jit(solution)/shard_map/ppermute | solution.py:17
  428.1 23.7 %collective-permute-start.21 = (bf16[1,3,64,640]{3,2,1,0:T(8,128)(2,1)S(1)}, bf16[1,3,64,640]{3,2,1,0:T(8,128)(2,1)S(1)}, u32[]{:S(2)}, u32[]{:S(2)}) collective-permute-start(bf16[1,3,64,640]{3,2,1,0:T(8,128)(2,1)S(1)} %get-tuple-element.84), channel_id=1, source_target_pairs={{12,0},{0,4},{4,8},{8,12},{13,1},{1,5},{5,9},{9,13},{14,2},{2,6},{... | collective-permute-start | bytes 737288 | tf_op jit(solution)/shard_map/ppermute | solution.py:17
  430.3 91.9 %collective-permute-start.13 = (bf16[320,1024]{1,0:T(8,128)(2,1)}, bf16[320,1024]{1,0:T(8,128)(2,1)}, u32[]{:S(2)}, u32[]{:S(2)}) collective-permute-start(bf16[320,1024]{1,0:T(8,128)(2,1)} %add_convert_fusion.5), channel_id=1, source_target_pairs={{0,2},{1,3},{2,0},{3,1},{4,6},{5,7},{6,4},{7,5},{8,10},{9,11},{10,... | collective-permute-start | bytes 1966088 | tf_op jit(solution)/shard_map/ppermute | solution.py:283
  453.7 2.7 copy-start.25
  453.7 2.7 copy-start.27
  522.1 10.2 %collective-permute-start.24 = (bf16[320,1024]{1,0:T(8,128)(2,1)}, bf16[320,1024]{1,0:T(8,128)(2,1)}, u32[]{:S(2)}, u32[]{:S(2)}) collective-permute-start(bf16[320,1024]{1,0:T(8,128)(2,1)} %dynamic-slice_convert_fusion), channel_id=1, source_target_pairs={{0,1},{1,0},{2,3},{3,2},{4,5},{5,4},{6,7},{7,6},{8,9},{9,8},{10,11... | collective-permute-start | bytes 1966088 | tf_op jit(solution)/shard_map/ppermute | solution.py:283
  524.5 11.0 %collective-permute-start.14 = (bf16[320,1024]{1,0:T(8,128)(2,1)}, bf16[320,1024]{1,0:T(8,128)(2,1)}, u32[]{:S(2)}, u32[]{:S(2)}) collective-permute-start(bf16[320,1024]{1,0:T(8,128)(2,1)} %add_convert_fusion.4), channel_id=1, source_target_pairs={{0,1},{1,0},{2,3},{3,2},{4,5},{5,4},{6,7},{7,6},{8,9},{9,8},{10,11... | collective-permute-start | bytes 1966088 | tf_op jit(solution)/shard_map/ppermute | solution.py:283
  534.1 2.8 copy-start.18
  534.1 16.7 %collective-permute-start.25 = (bf16[320,1024]{1,0:T(8,128)(2,1)S(1)}, bf16[320,1024]{1,0:T(8,128)(2,1)S(1)}, u32[]{:S(2)}, u32[]{:S(2)}) collective-permute-start(bf16[320,1024]{1,0:T(8,128)(2,1)S(1)} %add_convert_fusion.1), channel_id=1, source_target_pairs={{0,2},{1,3},{2,0},{3,1},{4,6},{5,7},{6,4},{7,5},{8,10},{9,11},{10,... | collective-permute-start | bytes 1966088 | tf_op jit(solution)/shard_map/ppermute | solution.py:283
  536.9 5.4 collective-permute-start.32
  540.3 10.8 %collective-permute-start.34 = (bf16[656,128]{1,0:T(8,128)(2,1)S(1)}, bf16[656,128]{1,0:T(8,128)(2,1)S(1)}, u32[]{:S(2)}, u32[]{:S(2)}) collective-permute-start(bf16[656,128]{1,0:T(8,128)(2,1)S(1)} %copy.81), channel_id=1, source_target_pairs={{0,16},{16,0},{1,17},{17,1},{2,18},{18,2},{3,19},{19,3},{4,20},{20... | collective-permute-start | bytes 503816 | tf_op jit(solution)/shard_map/ppermute | solution.py:283
  541.0 15.2 %collective-permute-start.33 = (bf16[2,128,656]{1,2,0:T(8,128)(2,1)S(1)}, bf16[2,128,656]{1,2,0:T(8,128)(2,1)S(1)}, u32[]{:S(2)}, u32[]{:S(2)}) collective-permute-start(bf16[2,128,656]{1,2,0:T(8,128)(2,1)S(1)} %copy.83), channel_id=1, source_target_pairs={{0,16},{16,0},{1,17},{17,1},{2,18},{18,2},{3,19},{19,3},{4,20},{20... | collective-permute-start | bytes 1007624 | tf_op jit(solution)/shard_map/ppermute | solution.py:283
  551.0 6.5 %collective-permute-start.26 = (bf16[320,1024]{1,0:T(8,128)(2,1)S(1)}, bf16[320,1024]{1,0:T(8,128)(2,1)S(1)}, u32[]{:S(2)}, u32[]{:S(2)}) collective-permute-start(bf16[320,1024]{1,0:T(8,128)(2,1)S(1)} %add_convert_fusion), channel_id=1, source_target_pairs={{0,1},{1,0},{2,3},{3,2},{4,5},{5,4},{6,7},{7,6},{8,9},{9,8},{10,11... | collective-permute-start | bytes 1966088 | tf_op jit(solution)/shard_map/ppermute | solution.py:283
  558.9 5.4 collective-permute-start.27
  560.1 4.5 collective-permute-start.28
  562.3 3.6 collective-permute-start.29
  566.0 37.0 %collective-permute-start.30 = (f32[2,256]{1,0:T(2,128)S(1)}, f32[2,256]{1,0:T(2,128)S(1)}, u32[]{:S(2)}, u32[]{:S(2)}) collective-permute-start(f32[2,256]{1,0:T(2,128)S(1)} %add_add_fusion), channel_id=1, source_target_pairs={{0,16},{16,0},{1,17},{17,1},{2,18},{18,2},{3,19},{19,3},{4,20},{20... | collective-permute-start | bytes 6152 | tf_op jit(solution)/shard_map/ppermute | solution.py:283
  598.2 5.7 collective-permute-start.31
  (13 other events, 22.1 us)
Sparse Core Ops, SparseCore 0:
  10.6 47.9 all-gather.3
  60.7 50.9 all-gather.7
  114.3 57.1 all-gather.5
  304.0 60.9 reduce-scatter.16
  368.6 64.8 reduce-scatter.12
  436.9 80.6 reduce-scatter.14
  532.4 64.4 reduce-scatter.18

commit v2 on v1

--- a/solution.py
+++ b/solution.py
@@ -1,6 +1,9 @@
+import functools
 import jax
 import jax.numpy as jnp
 from jax import lax
+from jax.experimental import pallas as pl
+from jax.experimental.pallas import tpu as pltpu
 from jax.sharding import PartitionSpec as P
 
 HD = 64
@@ -284,9 +287,26 @@
 
 
 def gather_weight(weight, dim):
-    half = weight.shape[dim] // lax.axis_size("seq")
-    mine = lax.dynamic_slice_in_dim(weight, lax.axis_index("seq") * half, half, dim)
-    return lax.all_gather(mine, ("ctx", "seq"), axis=dim, tiled=True)
+    group = lax.axis_size("ctx")
+    if group > 4:
+        return lax.all_gather(weight, "ctx", axis=dim, tiled=True)
+    me = lax.axis_index("ctx")
+    seq = lax.axis_index("seq")
+    half = weight.shape[dim] // 2
+    mine = lax.dynamic_slice_in_dim(weight, seq * half, half, dim)
+    near = jnp.stack([passed_along(mine, "ctx", k) for k in range(1, group)])
+    far = pair_swap(near, "seq", 1)
+    first = seq == 0
+    whole = jnp.concatenate(
+        [jnp.where(first, near, far), jnp.where(first, far, near)], axis=dim + 1
+    )
+    pieces = [weight] + [whole[k] for k in range(group - 1)]
+    stacked = jnp.stack(pieces)
+    ordered = [
+        lax.dynamic_index_in_dim(stacked, (me - j) % group, 0, keepdims=False)
+        for j in range(group)
+    ]
+    return jnp.concatenate(ordered, axis=dim)
 
 
 def gather_gains(gains):
@@ -303,7 +323,21 @@
 
 
 def reduce_weight(grad):
-    return lax.psum_scatter(grad, ("ctx", "seq"), scatter_dimension=1, tiled=True)
+    group = lax.axis_size("ctx")
+    me = lax.axis_index("ctx")
+    seq = lax.axis_index("seq")
+    a, rows, b = grad.shape
+    half = rows // group // 2
+    split = grad.reshape(a, group, 2, half, b)
+    keep = lax.dynamic_index_in_dim(split, seq, 2, keepdims=False)
+    give = lax.dynamic_index_in_dim(split, 1 - seq, 2, keepdims=False).astype(jnp.bfloat16)
+    both = keep + pair_swap(give, "seq", 1).astype(jnp.float32)
+    share = lax.dynamic_index_in_dim(both, me, 1, keepdims=False)
+    low_both = both.astype(jnp.bfloat16)
+    for k in range(1, group):
+        block = lax.dynamic_index_in_dim(low_both, (me + k) % group, 1, keepdims=False)
+        share = share + passed_along(block, "ctx", k).astype(jnp.float32)
+    return share.astype(jnp.bfloat16)
 
 
 def reduce_weight_rows(share):
@@ -371,32 +405,156 @@
     return (jnp.cos(angles), jnp.sin(angles))
 
 
-def attend(q, k, v, doc):
-    allowed = (doc[:, None] == doc[None, :])[None]
-    scores = jnp.einsum("ndi,ndj->nij", q, k, preferred_element_type=jnp.float32)
-    scores = jnp.where(allowed, scores, masked_score)
-    top = jnp.max(scores, axis=2)
-    weights = jnp.where(allowed, jnp.exp(scores - top[:, :, None]), 0.0)
-    total = jnp.sum(weights, axis=2)
-    out = jnp.einsum(
-        "ndj,nij->ndi", v, weights.astype(jnp.bfloat16), preferred_element_type=jnp.float32
-    )
-    return (out / total[:, None, :], top + jnp.log(total))
-
-
-def attend_back(q, k, v, doc, lse, out, grad):
-    allowed = (doc[:, None] == doc[None, :])[None]
-    delta = jnp.sum(grad.astype(jnp.float32) * out, axis=1)
-    scores = jnp.einsum("ndi,ndj->nij", q, k, preferred_element_type=jnp.float32)
-    probs = jnp.where(allowed, jnp.exp(scores - lse[:, :, None]), 0.0)
-    grad_v = jnp.einsum(
-        "ndi,nij->ndj", grad, probs.astype(jnp.bfloat16), preferred_element_type=jnp.float32
-    )
-    grad_probs = jnp.einsum("ndi,ndj->nij", grad, v, preferred_element_type=jnp.float32)
-    grad_s = (probs * (grad_probs - delta[:, :, None])).astype(jnp.bfloat16)
-    grad_q = jnp.einsum("ndj,nij->ndi", k, grad_s, preferred_element_type=jnp.float32)
-    grad_k = jnp.einsum("ndi,nij->ndj", q, grad_s, preferred_element_type=jnp.float32)
-    return (grad_q, grad_k, grad_v)
+def attend_kernel(tile, span_ref, q_ref, k_ref, v_ref, row_doc_ref, col_doc_ref, out_ref, lse_ref, keys_scr):
+    step = pl.program_id(0)
+
+    @pl.when(step == 0)
+    def _():
+        keys_scr[...] = k_ref[...].T
+
+    q = q_ref[...]
+    doc = row_doc_ref[...]
+    first, last = span_ref[0, step], span_ref[1, step]
+
+    def body(j, state):
+        top, total, out = state
+        at = pl.multiple_of(j * tile, tile)
+        s = jnp.dot(keys_scr[pl.ds(at, tile), :], q, preferred_element_type=jnp.float32)
+        allowed = col_doc_ref[pl.ds(at, tile), :] == doc
+        s = jnp.where(allowed, s, masked_score)
+        new_top = jnp.maximum(top, jnp.max(s, axis=0, keepdims=True))
+        e = jnp.where(allowed, jnp.exp(s - new_top), 0.0)
+        factor = jnp.exp(top - new_top)
+        total = total * factor + jnp.sum(e, axis=0, keepdims=True)
+        out = out * factor + jnp.dot(
+            v_ref[:, pl.ds(at, tile)], e.astype(jnp.bfloat16), preferred_element_type=jnp.float32
+        )
+        return (new_top, total, out)
+
+    width = q.shape[1]
+    state = (
+        jnp.full((1, width), masked_score, jnp.float32),
+        jnp.zeros((1, width), jnp.float32),
+        jnp.zeros((HD, width), jnp.float32),
+    )
+    top, total, out = lax.fori_loop(first, last, body, state)
+    out_ref[...] = out / total
+    lse_ref[...] = top + jnp.log(total)
+
+
+def attend_back_kernel(
+    tile, span_ref, q_ref, k_ref, v_ref, row_doc_ref, col_doc_ref, lse_ref, out_ref, grad_ref,
+    dq_ref, dk_ref, dv_ref, keys_scr, values_scr,
+):
+    step = pl.program_id(0)
+
+    @pl.when(step == 0)
+    def _():
+        keys_scr[...] = k_ref[...].T
+        values_scr[...] = v_ref[...].T
+        dk_ref[...] = jnp.zeros_like(dk_ref)
+        dv_ref[...] = jnp.zeros_like(dv_ref)
+
+    q = q_ref[...]
+    grad = grad_ref[...]
+    delta = jnp.sum(grad.astype(jnp.float32) * out_ref[...], axis=0, keepdims=True)
+    doc = row_doc_ref[...]
+    lse = lse_ref[...]
+    q_rows = q.T
+    grad_rows = grad.T
+    first, last = span_ref[0, step], span_ref[1, step]
+
+    def body(j, dq):
+        at = pl.multiple_of(j * tile, tile)
+        s = jnp.dot(keys_scr[pl.ds(at, tile), :], q, preferred_element_type=jnp.float32)
+        allowed = col_doc_ref[pl.ds(at, tile), :] == doc
+        p = jnp.where(allowed, jnp.exp(s - lse), 0.0)
+        dp = jnp.dot(values_scr[pl.ds(at, tile), :], grad, preferred_element_type=jnp.float32)
+        ds = (p * (dp - delta)).astype(jnp.bfloat16)
+        dv_ref[pl.ds(at, tile), :] += jnp.dot(
+            p.astype(jnp.bfloat16), grad_rows, preferred_element_type=jnp.float32
+        )
+        dk_ref[pl.ds(at, tile), :] += jnp.dot(ds, q_rows, preferred_element_type=jnp.float32)
+        return dq + jnp.dot(
+            k_ref[:, pl.ds(at, tile)], ds, preferred_element_type=jnp.float32
+        )
+
+    dq_ref[...] = lax.fori_loop(first, last, body, jnp.zeros(q.shape, jnp.float32))
+
+
+def tile_spans(lengths, tiles, tile):
+    ends = jnp.cumsum(lengths, dtype=jnp.int32)
+    starts = ends - lengths
+    low_row = jnp.arange(tiles, dtype=jnp.int32) * tile
+    high_row = low_row + (tile - 1)
+    low_doc = jnp.sum((low_row[:, None] >= ends[None, :]).astype(jnp.int32), axis=1)
+    high_doc = jnp.sum((high_row[:, None] >= ends[None, :]).astype(jnp.int32), axis=1)
+    slots = jnp.arange(lengths.shape[0], dtype=jnp.int32)[None, :]
+    begin = jnp.sum(jnp.where(slots == low_doc[:, None], starts[None, :], 0), axis=1)
+    finish = jnp.sum(jnp.where(slots == high_doc[:, None], ends[None, :], 0), axis=1)
+    return jnp.stack([begin // tile, (finish + (tile - 1)) // tile]).astype(jnp.int32)
+
+
+def head_specs(tile, total):
+    moving = pl.BlockSpec((HD, tile), lambda i, span: (0, i))
+    whole = pl.BlockSpec((HD, total), lambda i, span: (0, 0))
+    row = pl.BlockSpec((1, tile), lambda i, span: (0, i))
+    column = pl.BlockSpec((total, 1), lambda i, span: (0, 0))
+    return (moving, whole, row, column)
+
+
+def attend(q, k, v, doc, spans, tile):
+    total = q.shape[1]
+    moving, whole, row, column = head_specs(tile, total)
+    return pl.pallas_call(
+        functools.partial(attend_kernel, tile),
+        grid_spec=pltpu.PrefetchScalarGridSpec(
+            num_scalar_prefetch=1,
+            grid=(total // tile,),
+            in_specs=[moving, whole, whole, row, column],
+            out_specs=[moving, row],
+            scratch_shapes=[pltpu.VMEM((total, HD), jnp.bfloat16)],
+        ),
+        out_shape=[
+            jax.ShapeDtypeStruct((HD, total), jnp.float32),
+            jax.ShapeDtypeStruct((1, total), jnp.float32),
+        ],
+        compiler_params=pltpu.CompilerParams(vmem_limit_bytes=40 * 1024 * 1024),
+        cost_estimate=pl.CostEstimate(
+            flops=10 * total * total * HD, bytes_accessed=4 * total * HD, transcendentals=total * total
+        ),
+        name="attend",
+    )(spans, q, k, v, doc[None, :], doc[:, None])
+
+
+def attend_back(q, k, v, doc, spans, tile, lse, out, grad):
+    total = q.shape[1]
+    moving, whole, row, column = head_specs(tile, total)
+    tall = pl.BlockSpec((total, HD), lambda i, span: (0, 0))
+    dq, dk, dv = pl.pallas_call(
+        functools.partial(attend_back_kernel, tile),
+        grid_spec=pltpu.PrefetchScalarGridSpec(
+            num_scalar_prefetch=1,
+            grid=(total // tile,),
+            in_specs=[moving, whole, whole, row, column, row, moving, moving],
+            out_specs=[moving, tall, tall],
+            scratch_shapes=[
+                pltpu.VMEM((total, HD), jnp.bfloat16),
+                pltpu.VMEM((total, HD), jnp.bfloat16),
+            ],
+        ),
+        out_shape=[
+            jax.ShapeDtypeStruct((HD, total), jnp.float32),
+            jax.ShapeDtypeStruct((total, HD), jnp.float32),
+            jax.ShapeDtypeStruct((total, HD), jnp.float32),
+        ],
+        compiler_params=pltpu.CompilerParams(vmem_limit_bytes=40 * 1024 * 1024),
+        cost_estimate=pl.CostEstimate(
+            flops=20 * total * total * HD, bytes_accessed=4 * total * HD, transcendentals=total * total
+        ),
+        name="attend_back",
+    )(spans, q, k, v, doc[None, :], doc[:, None], lse, out, grad)
+    return (dq, dk.T, dv.T)
 
 
 def per_device(tokens, doc_lengths, norm_gains, w_qkv, w_out, w_in, w_down, cotangent):
@@ -411,9 +569,9 @@
     scale = HD ** (-0.5)
     gains = gather_gains(norm_gains).astype(jnp.float32)
     qkv_full = gather_weight(w_qkv, 1)
-    out_full = gather_weight(w_out, 1)
+    tail_full = gather_weight(jnp.concatenate([w_out, w_down], axis=0), 1)
+    out_full, down_full = (tail_full[:width], tail_full[width:])
     in_full = gather_weight(w_in, 1)
-    down_full = gather_weight(w_down, 1)
     doc_all, pos_all = token_layout(lengths, jnp.int32(0), rows * group)
     cos_all, sin_all = tables(pos_all)
     cos_here = lax.dynamic_slice_in_dim(cos_all, me * rows, rows, 1)
@@ -429,7 +587,10 @@
     blocks = jnp.stack([q, k, v], axis=1).reshape(group, each, 3, HD, rows)
     mine = jnp.concatenate(swap_blocks(blocks, 1), axis=-1)
     q, k, v = (mine[:, 0], mine[:, 1], mine[:, 2])
-    attn_float, lse = attend(q, k, v, doc_all)
+    q, k, v = (q.reshape(HD, -1), k.reshape(HD, -1), v.reshape(HD, -1))
+    tile = 512 if rows * group % 512 == 0 else 128
+    spans = tile_spans(lengths, rows * group // tile, tile)
+    attn_float, lse = attend(q, k, v, doc_all, spans, tile)
     parts = attn_float.astype(jnp.bfloat16).reshape(each, HD, group, rows).transpose(2, 0, 1, 3)
     attn_low = jnp.concatenate(swap_blocks(parts, -1), axis=0).reshape(width, rows)
 
@@ -452,15 +613,15 @@
     )
     grad_input_two = head_sum(partial_two)
     grad_down = jnp.einsum(
-        "tf,td->fd", mixed_low, grad_rows, preferred_element_type=jnp.float32
-    ).astype(jnp.bfloat16)
+        "tf,td->df", mixed_low, grad_rows, preferred_element_type=jnp.float32
+    )
     grad_in = jnp.einsum(
         "td,tcf->cdf", input_two, grad_gate_up, preferred_element_type=jnp.float32
-    ).astype(jnp.bfloat16)
+    )
     grad_input_two, grad_down, grad_in = lax.optimization_barrier(
         (grad_input_two, grad_down, grad_in)
     )
-    share_down = reduce_weight(grad_down)
+    share_down = reduce_weight(grad_down[None])
     share_in = reduce_weight(grad_in)
     result = (resid_one + head_sum(partial_ffn)).astype(jnp.bfloat16)
     grad_norm_two, gain_grad_two = norm_back(grad_input_two, normed_two, inverse_two, gains[1])
@@ -473,14 +634,16 @@
         swap_blocks(grad_attn.reshape(group, each, HD, rows), 1), axis=-1
     )
     grad_out = jnp.einsum(
-        "nt,td->nd", attn_low, grad_branch, preferred_element_type=jnp.float32
-    ).astype(jnp.bfloat16)
+        "nt,td->dn", attn_low, grad_branch, preferred_element_type=jnp.float32
+    )
     grad_mine, grad_out = lax.optimization_barrier((grad_mine, grad_out))
-    share_out = reduce_weight(grad_out)
-    grad_q, grad_k, grad_v = attend_back(q, k, v, doc_all, lse, attn_float, grad_mine)
+    share_out = reduce_weight(grad_out[None])
+    grad_q, grad_k, grad_v = attend_back(
+        q, k, v, doc_all, spans, tile, lse, attn_float, grad_mine.reshape(HD, -1)
+    )
     grad_q = turn(grad_q, cos_all, -sin_all) * scale
     grad_k = turn(grad_k, cos_all, -sin_all)
-    back = jnp.stack([grad_q, grad_k, grad_v], axis=1).astype(jnp.bfloat16)
+    back = jnp.stack([grad_q, grad_k, grad_v]).astype(jnp.bfloat16)
     back = back.reshape(each, 3, HD, group, rows).transpose(3, 0, 1, 2, 4)
     grad_raw = jnp.concatenate(swap_blocks(back, -1), axis=0)
     grad_raw = grad_raw.transpose(1, 0, 2, 3).reshape(3, width, rows)
@@ -489,9 +652,6 @@
     )
     grad_qkv = jnp.einsum(
         "td,cnt->cdn", input_one, grad_raw, preferred_element_type=jnp.float32
-    ).astype(jnp.bfloat16)
-    partial_one, grad_qkv, share_down, share_in, share_out = lax.optimization_barrier(
-        (partial_one, grad_qkv, share_down, share_in, share_out)
     )
     share_qkv = reduce_weight(grad_qkv)
     grad_input_one = head_sum(partial_one)
@@ -503,15 +663,15 @@
         grad_tokens[None],
         total_gains,
         reduce_weight_rows(share_qkv),
-        reduce_weight_rows(share_out),
+        reduce_weight_rows(share_out)[0].T,
         reduce_weight_rows(share_in),
-        reduce_weight_rows(share_down),
+        reduce_weight_rows(share_down)[0].T,
     )
 
 
 def solution(mesh):
     heads = 1024 // HD // mesh.shape["head"]
-    body = per_device if heads % mesh.shape["ctx"] == 0 else per_device_ring
+    body = per_device if heads == mesh.shape["ctx"] else per_device_ring
     return jax.shard_map(
         body,
         mesh=mesh,

time: 619 us -> 497 us (0.80)
  matrix products: 96.5 us -> 34.3 us
  waiting for transfers between devices: 225 us -> 169 us
  starting transfers between devices: 37 us -> 87.8 us
  Pallas kernels: 0 us -> 32.4 us
  other arithmetic: 92.9 us -> 63.7 us
  blocking collectives: 28.2 us -> 0 us
  local copies, waits for them, and re-layouts: 117 us -> 102 us
  between operations: 15.6 us -> 2.58 us
    unnamed x11 -> x0, waiting for transfers between devices: 86.3 us -> none
    ppermute x18 -> x39, waiting for transfers between devices: 53.3 us -> 125 us  [passed_along(): return lax.ppermute(block, axis, route)]
    dot_general x8 -> x2, matrix products: 67.8 us -> 7.58 us  [the longest x1 5.99 us: per_device(): jnp.einsum('tf,td->df', mixed_low, grad_rows, preferred_element_type=jnp....]
    dynamic_slice x4 -> x24, local copies, waits for them, and re-layouts: 3.43 us -> 43.8 us  [the longest x4 17.2 us: reduce_weight(): keep = lax.dynamic_index_in_dim(split, seq, 2, keepdims=False)]
    all_gather x3 -> x0, waiting for transfers between devices: 39.2 us -> none  [gather_weight(): return lax.all_gather(mine, ('ctx', 'seq'), axis=dim, tiled=True)]
    pallas_call x0 -> x2, Pallas kernels: none -> 32.4 us  [the longest x1 17.7 us: attend_back(): pl.pallas_call(functools.partial(attend_back_kernel, tile), grid_spec=plt...]
    ppermute x18 -> x39, starting transfers between devices: 23.8 us -> 56 us  [passed_along(): return lax.ppermute(block, axis, route)]
    unnamed x85 -> x130, local copies, waits for them, and re-layouts: 47.6 us -> 16 us
  transfers between devices with their start and end apart: 42 -> 63, of which waited for: 20 -> 23; matrix products, arithmetic and copies ran while one was open for 42% -> 35% of each run, Pallas kernels for 0% -> 4%
where the time goes in v2:
time: 497 us; the launch traced here: 493 us
  waiting for transfers between devices  169 us (34%)
  local copies, waits for them, and re-layouts  102 us (21%)
  starting transfers between devices  87.8 us (18%)
  other arithmetic  63.7 us (13%)
  matrix products  34.3 us (7%)
  Pallas kernels  32.4 us (7%)
    ppermute x39, waiting for transfers between devices, passed_along(): return lax.ppermute(block, axis, route)  125 us
    ppermute x39, starting transfers between devices, passed_along(): return lax.ppermute(block, axis, route)  56 us
    ppermute x24, waiting for transfers between devices, pair_swap(): return lax.ppermute(block, axis, [(i, i ^ mask) for i in range(size)])  44.1 us
    ppermute x24, starting transfers between devices, pair_swap(): return lax.ppermute(block, axis, [(i, i ^ mask) for i in range(size)])  31.9 us
    pallas_call x1, Pallas kernels, attend_back(): pl.pallas_call(functools.partial(attend_back_kernel, tile), grid_spec=plt...  17.7 us
    dynamic_slice x4, local copies, waits for them, and re-layouts, reduce_weight(): keep = lax.dynamic_index_in_dim(split, seq, 2, keepdims=False)  17.2 us
    unnamed x130, local copies, waits for them, and re-layouts  16 us
    pallas_call x1, Pallas kernels, attend(): pl.pallas_call(functools.partial(attend_kernel, tile), grid_spec=pltpu.Pr...  14.8 us
  transfers between devices with their start and end apart: 63, of which 23 were waited for; matrix products, arithmetic and copies ran while one was open for 35% of the time, Pallas kernels for 4%

profile of v2, /device:TPU:0, one launch (start us, length us, event | category | flops | bytes accessed | tf_op | source)
XLA Modules:
  0.0 492.7 jit_solution(2081600219281733611)
XLA Ops:
  0.6 3.1 collective-permute-start.4
  3.7 2.6 collective-permute-start.5
  14.0 6.2 %multiply_cosine_fusion = (f32[32,2560]{0,1:T(8,128)}, f32[32,2560]{0,1:T(8,128)}) fusion(f32[2560]{0:T(1024)S(1)} %subtract_convert_fusion.1, f32[32]{0:T(128)S(1)} %negate_power_fusion), kind=kLoop, calls=%fused_computation.47 | loop fusion | flops 81920 | bytes 665728 | tf_op jit(solution)/shard_map/cos | solution.py:405
  26.4 3.1 collective-permute-start.6
  37.2 12.5 %collective-permute-done.14 = bf16[912,128]{1,0:T(8,128)(2,1)S(1)} collective-permute-done((bf16[912,128]{1,0:T(8,128)(2,1)}, bf16[912,128]{1,0:T(8,128)(2,1)S(1)}, u32[]{:S(2)}, u32[]{:S(2)}) %collective-permute-start.14) | collective-permute-done | bytes 233504 | tf_op jit(solution)/shard_map/ppermute | solution.py:20
  59.3 2.9 fusion.73
  63.7 2.7 collective-permute-start.8
  71.2 16.9 %collective-permute-done.8 = bf16[1,3,64,640]{3,2,1,0:T(8,128)(2,1)S(1)} collective-permute-done((bf16[1,3,64,640]{3,2,1,0:T(8,128)(2,1)S(1)}, bf16[1,3,64,640]{3,2,1,0:T(8,128)(2,1)S(1)}, u32[]{:S(2)}, u32[]{:S(2)}) %collective-permute-start.8) | collective-permute-done | bytes 245792 | tf_op jit(solution)/shard_map/ppermute | solution.py:20
  88.5 14.8 %attend.1 = (f32[64,2560]{1,0:T(8,128)S(1)}, f32[1,2560]{1,0:T(1,128)S(1)}) custom-call(s32[2,5]{1,0:T(2,128)S(1)} %pad_add_fusion.span_ref, bf16[64,2560]{1,0:T(8,128)(2,1)S(1)} %get-tuple-element.92.q_ref, bf16[64,2560]{1,0:T(8,128)(2,1)S(1)} %get-tuple-element.91.k_ref, bf16[64,2560]{1,0:T(8,128)(2,1)S(1)} %get-tuple-element.90.v_ref, ...), custom_call_target="tpu_custom_call" | custom-call | flops 4194304000 | bytes 655360 | tf_op jit(solution)/shard_map/attend/pallas_call | solution.py:509
  105.9 2.2 constant_dynamic-slice_fusion.28
  108.3 2.1 collective-permute-start.10
  110.5 2.2 collective-permute-done.12
  112.7 3.8 collective-permute-done.11
  122.8 2.2 collective-permute-start.20
  125.0 6.9 %collective-permute-done.22 = bf16[2,128,656]{1,2,0:T(8,128)(2,1)} collective-permute-done((bf16[2,128,656]{1,2,0:T(8,128)(2,1)}, bf16[2,128,656]{1,2,0:T(8,128)(2,1)}, u32[]{:S(2)}, u32[]{:S(2)}) %collective-permute-start.22) | collective-permute-done | bytes 335904 | tf_op jit(solution)/shard_map/ppermute | solution.py:20
  131.9 21.4 %collective-permute-done.21 = bf16[2,128,656]{1,2,0:T(8,128)(2,1)} collective-permute-done((bf16[2,128,656]{1,2,0:T(8,128)(2,1)}, bf16[2,128,656]{1,2,0:T(8,128)(2,1)}, u32[]{:S(2)}, u32[]{:S(2)}) %collective-permute-start.21) | collective-permute-done | bytes 335904 | tf_op jit(solution)/shard_map/ppermute | solution.py:20
  153.2 2.2 pad_maximum_fusion.11
  155.5 4.8 collective-permute-start.23
  160.3 2.6 add_convert_fusion.7
  164.4 3.0 fusion.77
  167.3 12.1 %collective-permute-done.18 = bf16[320,1024]{1,0:T(8,128)(2,1)} collective-permute-done((bf16[320,1024]{1,0:T(8,128)(2,1)}, bf16[320,1024]{1,0:T(8,128)(2,1)}, u32[]{:S(2)}, u32[]{:S(2)}) %collective-permute-start.18) | collective-permute-done | bytes 655392 | tf_op jit(solution)/shard_map/ppermute | solution.py:286
  186.3 2.5 fusion.129
  188.8 4.0 fusion.119
  194.3 2.2 convolution_bitcast_fusion.4
  199.0 4.2 fusion.85
  207.0 6.0 %convolution_bitcast_fusion.2 = f32[1024,656]{0,1:T(8,128)} fusion(bf16[1,640,1024]{2,1,0:T(8,128)(2,1)S(1)} %copy-done.40, f32[640,2,656]{0,2,1:T(8,128)S(1)} %copy-done.22), kind=kOutput, calls=%fused_computation.53 | convolution fusion | flops 887541760 | bytes 7356416 | tf_op jit(solution)/shard_map/tf,td->df/dot_general | solution.py:615
  213.9 9.2 %collective-permute-done.28 = bf16[320,1024]{1,0:T(8,128)(2,1)S(1)} collective-permute-done((bf16[320,1024]{1,0:T(8,128)(2,1)S(1)}, bf16[320,1024]{1,0:T(8,128)(2,1)S(1)}, u32[]{:S(2)}, u32[]{:S(2)}) %collective-permute-start.28) | collective-permute-done | bytes 655392 | tf_op jit(solution)/shard_map/ppermute | solution.py:286
  223.5 4.8 convolution_bitcast_fusion
  228.3 7.7 %collective-permute-done.25 = bf16[320,1024]{1,0:T(8,128)(2,1)S(1)} collective-permute-done((bf16[320,1024]{1,0:T(8,128)(2,1)S(1)}, bf16[320,1024]{1,0:T(8,128)(2,1)S(1)}, u32[]{:S(2)}, u32[]{:S(2)}) %collective-permute-start.25) | collective-permute-done | bytes 655392 | tf_op jit(solution)/shard_map/ppermute | solution.py:286
  243.7 2.7 collective-permute-start.31
  248.4 8.4 %reshape.554 = f32[2,4,2,128,656]{3,2,1,4,0:T(2,128)} reshape(f32[2,1024,656]{1,2,0:T(8,128)} %convolution_bitcast_fusion) | data formatting | bytes 10747904 | tf_op jit(solution)/shard_map/reshape | solution.py:331
  256.8 4.9 %constant_dynamic-slice_fusion.6 = bf16[2,4,1,128,656]{3,2,1,4,0:T(2,128)(2,1)S(1)} fusion(f32[2,4,2,128,656]{3,2,1,4,0:T(2,128)} %reshape.554, s32[]{:T(128)S(6)} %select_n.501), kind=kLoop, calls=%fused_computation.316 | loop fusion | bytes 2686980 | tf_op jit(solution)/shard_map/jit(dynamic_index_in_dim)/dynamic_slice | solution.py:333
  264.8 4.9 reshape_broadcast_in_dim.7
  269.7 3.0 constant_dynamic-slice_fusion.4
  273.6 6.9 %constant_dynamic-slice_fusion.7 = f32[2,4,1,128,656]{3,2,1,4,0:T(1,128)} fusion(f32[2,4,2,128,656]{3,2,1,4,0:T(2,128)} %reshape.554, s32[]{:T(128)S(6)} %select_n.500), kind=kLoop, calls=%fused_computation.317 | loop fusion | bytes 5373956 | tf_op jit(solution)/shard_map/jit(dynamic_index_in_dim)/dynamic_slice | solution.py:332
  288.0 17.7 %attend_back.1 = (f32[64,2560]{1,0:T(8,128)S(1)}, f32[2560,64]{1,0:T(8,128)S(1)}, f32[2560,64]{1,0:T(8,128)S(1)}) custom-call(s32[2,5]{1,0:T(2,128)S(1)} %pad_add_fusion.span_ref, bf16[64,2560]{1,0:T(8,128)(2,1)S(1)} %copy-done.6, bf16[64,2560]{1,0:T(8,128)(2,1)S(1)} %copy-done.4, bf16[64,2560]{1,0:T(8,128)(2,1)S(1)} %copy-done.2, ...), custom_call_target="tpu_custom_call" | custom-call | flops 8388608000 | bytes 655360 | tf_op jit(solution)/shard_map/attend_back/pallas_call | solution.py:534
  308.0 5.8 %fusion.62 = (f32[32,2560]{0,1:T(8,128)S(1)}, f32[32,2560]{0,1:T(8,128)S(1)}, bf16[32,2560]{0,1:T(8,128)(2,1)S(1)}, bf16[32,2560]{0,1:T(8,128)(2,1)S(1)}) fusion(f32[64,2560]{0,1:T(8,128)S(1)} %copy.88, f32[2560]{0:T(1024)S(1)} %subtract_convert_fusion.1, f32[32]{0:T(128)S(1)} %negate_power_fusion, f32[64,2560]{0,1:T(8,128)S(1)} %bitcast.472), kind=kLoop, calls=%fused_computation.116 | loop fusion | flops 1310720 | bytes 2304128 | tf_op jit(solution)/shard_map/sub | solution.py:398
  316.3 2.1 copy.93
  324.5 2.3 constant_dynamic-slice_fusion.5
  328.1 6.7 %collective-permute-start.48 = (bf16[1,4,128,256]{3,2,1,0:T(8,128)(2,1)S(1)}, bf16[1,4,128,256]{3,2,1,0:T(8,128)(2,1)}, u32[]{:S(2)}, u32[]{:S(2)}) collective-permute-start(bf16[1,4,128,256]{3,2,1,0:T(8,128)(2,1)S(1)} %fusion.137), channel_id=1, source_target_pairs={{0,16},{16,0},{1,17},{17,1},{2,18},{18,2},{3,19},{19,3},{4,20},{20... | collective-permute-start | bytes 786440 | tf_op jit(solution)/shard_map/ppermute | solution.py:286
  334.8 6.5 %collective-permute-done.34 = bf16[1,3,64,640]{3,2,1,0:T(8,128)(2,1)} collective-permute-done((bf16[1,3,64,640]{3,2,1,0:T(8,128)(2,1)}, bf16[1,3,64,640]{3,2,1,0:T(8,128)(2,1)}, u32[]{:S(2)}, u32[]{:S(2)}) %collective-permute-start.34) | collective-permute-done | bytes 245792 | tf_op jit(solution)/shard_map/ppermute | solution.py:20
  344.0 2.8 convolution_bitcast_fusion.3
  346.8 3.2 convolution_bitcast_fusion.1
  350.0 5.8 %reshape.553 = f32[3,4,2,128,256]{3,2,1,4,0:T(2,128)} reshape(f32[3,1024,256]{1,2,0:T(8,128)} %convolution_bitcast_fusion.1) | data formatting | bytes 6291456 | tf_op jit(solution)/shard_map/reshape | solution.py:331
  355.8 3.3 constant_dynamic-slice_fusion.12
  359.1 2.9 copy.113
  362.0 4.5 constant_dynamic-slice_fusion.13
  366.5 3.5 copy.97
  370.0 2.3 dynamic-slice_convert_fusion
  376.4 3.3 collective-permute-start.50
  384.4 2.4 collective-permute-done.49
  387.8 6.5 %collective-permute-start.52 = (bf16[1,128,256]{1,2,0:T(8,128)(2,1)S(1)}, bf16[1,128,256]{1,2,0:T(8,128)(2,1)S(1)}, u32[]{:S(2)}, u32[]{:S(2)}) collective-permute-start(bf16[1,128,256]{1,2,0:T(8,128)(2,1)S(1)} %fusion.144), channel_id=1, source_target_pairs={{0,16},{16,0},{1,17},{17,1},{2,18},{18,2},{3,19},{19,3},{4,20},{20... | collective-permute-start | bytes 196616 | tf_op jit(solution)/shard_map/ppermute | solution.py:286
  399.9 2.6 collective-permute-done.61
  402.7 9.2 %collective-permute-done.60 = bf16[1,128,656]{1,2,0:T(8,128)(2,1)S(1)} collective-permute-done((bf16[1,128,656]{1,2,0:T(8,128)(2,1)S(1)}, bf16[1,128,656]{1,2,0:T(8,128)(2,1)S(1)}, u32[]{:S(2)}, u32[]{:S(2)}) %collective-permute-start.60) | collective-permute-done | bytes 167968 | tf_op jit(solution)/shard_map/ppermute | solution.py:20
  414.2 7.5 %collective-permute-done.62 = bf16[1,128,656]{1,2,0:T(8,128)(2,1)S(1)} collective-permute-done((bf16[1,128,656]{1,2,0:T(8,128)(2,1)S(1)}, bf16[1,128,656]{1,2,0:T(8,128)(2,1)S(1)}, u32[]{:S(2)}, u32[]{:S(2)}) %collective-permute-start.62) | collective-permute-done | bytes 167968 | tf_op jit(solution)/shard_map/ppermute | solution.py:286
  422.9 3.8 collective-permute-start.46
  426.7 2.3 collective-permute-start.45
  430.8 3.9 collective-permute-start.56
  436.0 12.7 %collective-permute-done.45 = bf16[3,128,256]{2,1,0:T(8,128)(2,1)S(1)} collective-permute-done((bf16[3,128,256]{2,1,0:T(8,128)(2,1)S(1)}, bf16[3,128,256]{2,1,0:T(8,128)(2,1)S(1)}, u32[]{:S(2)}, u32[]{:S(2)}) %collective-permute-start.45) | collective-permute-done | bytes 196640 | tf_op jit(solution)/shard_map/ppermute | solution.py:20
  449.4 19.5 %collective-permute-done.55 = bf16[2,128,656]{1,2,0:T(8,128)(2,1)S(1)} collective-permute-done((bf16[2,128,656]{1,2,0:T(8,128)(2,1)S(1)}, bf16[2,128,656]{1,2,0:T(8,128)(2,1)S(1)}, u32[]{:S(2)}, u32[]{:S(2)}) %collective-permute-start.55) | collective-permute-done | bytes 335904 | tf_op jit(solution)/shard_map/ppermute | solution.py:20
  471.2 5.1 %collective-permute-done.57 = bf16[2,128,656]{1,2,0:T(8,128)(2,1)S(1)} collective-permute-done((bf16[2,128,656]{1,2,0:T(8,128)(2,1)S(1)}, bf16[2,128,656]{1,2,0:T(8,128)(2,1)S(1)}, u32[]{:S(2)}, u32[]{:S(2)}) %collective-permute-start.57) | collective-permute-done | bytes 335904 | tf_op jit(solution)/shard_map/ppermute | solution.py:286
  478.9 3.7 collective-permute-start.40
  484.6 3.4 collective-permute-done.39
  488.7 2.4 fusion.71
  (362 shorter events, 130.8 us)
Async XLA Ops:
  0.6 30.9 %collective-permute-start.4 = (bf16[2,256]{1,0:T(2,128)(2,1)}, bf16[2,256]{1,0:T(2,128)(2,1)S(1)}, u32[]{:S(2)}, u32[]{:S(2)}) collective-permute-start(bf16[2,256]{1,0:T(2,128)(2,1)} %param.10), channel_id=1, source_target_pairs={{12,0},{0,4},{4,8},{8,12},{13,1},{1,5},{5,9},{9,13},{14,2},{2,6},{... | collective-permute-start | bytes 3080 | tf_op jit(solution)/shard_map/ppermute | solution.py:20
  3.7 29.4 %collective-permute-start.5 = (bf16[2,256]{1,0:T(2,128)(2,1)}, bf16[2,256]{1,0:T(2,128)(2,1)S(1)}, u32[]{:S(2)}, u32[]{:S(2)}) collective-permute-start(bf16[2,256]{1,0:T(2,128)(2,1)} %param.10), channel_id=1, source_target_pairs={{8,0},{12,4},{0,8},{4,12},{9,1},{13,5},{1,9},{5,13},{10,2},{14,6},... | collective-permute-start | bytes 3080 | tf_op jit(solution)/shard_map/ppermute | solution.py:20
  7.9 18.4 %collective-permute-start.2 = (bf16[3,128,256]{2,1,0:T(8,128)(2,1)}, bf16[3,128,256]{2,1,0:T(8,128)(2,1)S(1)}, u32[]{:S(2)}, u32[]{:S(2)}) collective-permute-start(bf16[3,128,256]{2,1,0:T(8,128)(2,1)} %constant_dynamic-slice_fusion.38), channel_id=1, source_target_pairs={{4,0},{8,4},{12,8},{0,12},{5,1},{9,5},{13,9},{1,13},{6,2},{10,6},{... | collective-permute-start | bytes 589832 | tf_op jit(solution)/shard_map/ppermute | solution.py:20
  9.3 20.2 %collective-permute-start.1 = (bf16[3,128,256]{2,1,0:T(8,128)(2,1)}, bf16[3,128,256]{2,1,0:T(8,128)(2,1)}, u32[]{:S(2)}, u32[]{:S(2)}) collective-permute-start(bf16[3,128,256]{2,1,0:T(8,128)(2,1)} %constant_dynamic-slice_fusion.38), channel_id=1, source_target_pairs={{8,0},{12,4},{0,8},{4,12},{9,1},{13,5},{1,9},{5,13},{10,2},{14,6},... | collective-permute-start | bytes 589832 | tf_op jit(solution)/shard_map/ppermute | solution.py:20
  9.5 21.0 %collective-permute-start = (bf16[3,128,256]{2,1,0:T(8,128)(2,1)}, bf16[3,128,256]{2,1,0:T(8,128)(2,1)}, u32[]{:S(2)}, u32[]{:S(2)}) collective-permute-start(bf16[3,128,256]{2,1,0:T(8,128)(2,1)} %constant_dynamic-slice_fusion.38), channel_id=1, source_target_pairs={{12,0},{0,4},{4,8},{8,12},{13,1},{1,5},{5,9},{9,13},{14,2},{2,6},{... | collective-permute-start | bytes 589832 | tf_op jit(solution)/shard_map/ppermute | solution.py:20
  26.4 8.7 %collective-permute-start.6 = (bf16[2,256]{1,0:T(2,128)(2,1)S(1)}, bf16[2,256]{1,0:T(2,128)(2,1)S(1)}, u32[]{:S(2)}, u32[]{:S(2)}) collective-permute-start(bf16[2,256]{1,0:T(2,128)(2,1)S(1)} %copy-done.60), channel_id=1, source_target_pairs={{4,0},{8,4},{12,8},{0,12},{5,1},{9,5},{13,9},{1,13},{6,2},{10,6},{... | collective-permute-start | bytes 3080 | tf_op jit(solution)/shard_map/ppermute | solution.py:20
  29.4 7.7 %collective-permute-start.15 = (bf16[912,128]{1,0:T(8,128)(2,1)}, bf16[912,128]{1,0:T(8,128)(2,1)S(1)}, u32[]{:S(2)}, u32[]{:S(2)}) collective-permute-start(bf16[912,128]{1,0:T(8,128)(2,1)} %constant_dynamic-slice_fusion.24), channel_id=1, source_target_pairs={{4,0},{8,4},{12,8},{0,12},{5,1},{9,5},{13,9},{1,13},{6,2},{10,6},{... | collective-permute-start | bytes 700424 | tf_op jit(solution)/shard_map/ppermute | solution.py:20
  30.5 19.2 %collective-permute-start.14 = (bf16[912,128]{1,0:T(8,128)(2,1)}, bf16[912,128]{1,0:T(8,128)(2,1)S(1)}, u32[]{:S(2)}, u32[]{:S(2)}) collective-permute-start(bf16[912,128]{1,0:T(8,128)(2,1)} %constant_dynamic-slice_fusion.24), channel_id=1, source_target_pairs={{8,0},{12,4},{0,8},{4,12},{9,1},{13,5},{1,9},{5,13},{10,2},{14,6},... | collective-permute-start | bytes 700424 | tf_op jit(solution)/shard_map/ppermute | solution.py:20
  31.6 20.5 %collective-permute-start.3 = (bf16[3,3,128,256]{3,2,1,0:T(8,128)(2,1)S(1)}, bf16[3,3,128,256]{3,2,1,0:T(8,128)(2,1)S(1)}, u32[]{:S(2)}, u32[]{:S(2)}) collective-permute-start(bf16[3,3,128,256]{3,2,1,0:T(8,128)(2,1)S(1)} %pad_maximum_fusion.18), channel_id=1, source_target_pairs={{0,16},{16,0},{1,17},{17,1},{2,18},{18,2},{3,19},{19,3},{4,20},{20... | collective-permute-start | bytes 1769480 | tf_op jit(solution)/shard_map/ppermute | solution.py:286
  33.2 16.5 %collective-permute-start.13 = (bf16[912,128]{1,0:T(8,128)(2,1)}, bf16[912,128]{1,0:T(8,128)(2,1)S(1)}, u32[]{:S(2)}, u32[]{:S(2)}) collective-permute-start(bf16[912,128]{1,0:T(8,128)(2,1)} %constant_dynamic-slice_fusion.24), channel_id=1, source_target_pairs={{12,0},{0,4},{4,8},{8,12},{13,1},{1,5},{5,9},{9,13},{14,2},{2,6},{... | collective-permute-start | bytes 700424 | tf_op jit(solution)/shard_map/ppermute | solution.py:20
  50.6 17.8 %collective-permute-start.16 = (bf16[3,912,128]{2,1,0:T(8,128)(2,1)}, bf16[3,912,128]{2,1,0:T(8,128)(2,1)}, u32[]{:S(2)}, u32[]{:S(2)}) collective-permute-start(bf16[3,912,128]{2,1,0:T(8,128)(2,1)} %pad_maximum_fusion.16), channel_id=1, source_target_pairs={{0,16},{16,0},{1,17},{17,1},{2,18},{18,2},{3,19},{19,3},{4,20},{20... | collective-permute-start | bytes 2101256 | tf_op jit(solution)/shard_map/ppermute | solution.py:286
  63.7 7.5 %collective-permute-start.9 = (bf16[1,3,64,640]{3,2,1,0:T(8,128)(2,1)S(1)}, bf16[1,3,64,640]{3,2,1,0:T(8,128)(2,1)S(1)}, u32[]{:S(2)}, u32[]{:S(2)}) collective-permute-start(bf16[1,3,64,640]{3,2,1,0:T(8,128)(2,1)S(1)} %get-tuple-element.98), channel_id=1, source_target_pairs={{4,0},{8,4},{12,8},{0,12},{5,1},{9,5},{13,9},{1,13},{6,2},{10,6},{... | collective-permute-start | bytes 737288 | tf_op jit(solution)/shard_map/ppermute | solution.py:20
  63.7 24.3 %collective-permute-start.8 = (bf16[1,3,64,640]{3,2,1,0:T(8,128)(2,1)S(1)}, bf16[1,3,64,640]{3,2,1,0:T(8,128)(2,1)S(1)}, u32[]{:S(2)}, u32[]{:S(2)}) collective-permute-start(bf16[1,3,64,640]{3,2,1,0:T(8,128)(2,1)S(1)} %get-tuple-element.99), channel_id=1, source_target_pairs={{8,0},{12,4},{0,8},{4,12},{9,1},{13,5},{1,9},{5,13},{10,2},{14,6},... | collective-permute-start | bytes 737288 | tf_op jit(solution)/shard_map/ppermute | solution.py:20
  66.5 21.6 %collective-permute-start.7 = (bf16[1,3,64,640]{3,2,1,0:T(8,128)(2,1)S(1)}, bf16[1,3,64,640]{3,2,1,0:T(8,128)(2,1)S(1)}, u32[]{:S(2)}, u32[]{:S(2)}) collective-permute-start(bf16[1,3,64,640]{3,2,1,0:T(8,128)(2,1)S(1)} %get-tuple-element.100), channel_id=1, source_target_pairs={{12,0},{0,4},{4,8},{8,12},{13,1},{1,5},{5,9},{9,13},{14,2},{2,6},{... | collective-permute-start | bytes 737288 | tf_op jit(solution)/shard_map/ppermute | solution.py:20
  108.1 4.6 collective-permute-start.12
  108.2 8.3 %collective-permute-start.11 = (bf16[1,64,640]{2,1,0:T(8,128)(2,1)S(1)}, bf16[1,64,640]{2,1,0:T(8,128)(2,1)S(1)}, u32[]{:S(2)}, u32[]{:S(2)}) collective-permute-start(bf16[1,64,640]{2,1,0:T(8,128)(2,1)S(1)} %bitcast.526), channel_id=1, source_target_pairs={{8,0},{12,4},{0,8},{4,12},{9,1},{13,5},{1,9},{5,13},{10,2},{14,6},... | collective-permute-start | bytes 245768 | tf_op jit(solution)/shard_map/ppermute | solution.py:20
  108.3 8.2 %collective-permute-start.10 = (bf16[1,64,640]{2,1,0:T(8,128)(2,1)S(1)}, bf16[1,64,640]{2,1,0:T(8,128)(2,1)S(1)}, u32[]{:S(2)}, u32[]{:S(2)}) collective-permute-start(bf16[1,64,640]{2,1,0:T(8,128)(2,1)S(1)} %bitcast.527), channel_id=1, source_target_pairs={{12,0},{0,4},{4,8},{8,12},{13,1},{1,5},{5,9},{9,13},{14,2},{2,6},{... | collective-permute-start | bytes 245768 | tf_op jit(solution)/shard_map/ppermute | solution.py:20
  120.3 40.0 %collective-permute-start.17 = (bf16[320,1024]{1,0:T(8,128)(2,1)}, bf16[320,1024]{1,0:T(8,128)(2,1)}, u32[]{:S(2)}, u32[]{:S(2)}) collective-permute-start(bf16[320,1024]{1,0:T(8,128)(2,1)} %dynamic-slice_convert_fusion.3), channel_id=1, source_target_pairs={{0,1},{1,0},{2,3},{3,2},{4,5},{5,4},{6,7},{7,6},{8,9},{9,8},{10,11... | collective-permute-start | bytes 1966088 | tf_op jit(solution)/shard_map/ppermute | solution.py:286
  121.1 10.8 %collective-permute-start.22 = (bf16[2,128,656]{1,2,0:T(8,128)(2,1)}, bf16[2,128,656]{1,2,0:T(8,128)(2,1)}, u32[]{:S(2)}, u32[]{:S(2)}) collective-permute-start(bf16[2,128,656]{1,2,0:T(8,128)(2,1)} %constant_dynamic-slice_fusion.23), channel_id=1, source_target_pairs={{4,0},{8,4},{12,8},{0,12},{5,1},{9,5},{13,9},{1,13},{6,2},{10,6},{... | collective-permute-start | bytes 1007624 | tf_op jit(solution)/shard_map/ppermute | solution.py:20
  122.7 30.6 %collective-permute-start.21 = (bf16[2,128,656]{1,2,0:T(8,128)(2,1)}, bf16[2,128,656]{1,2,0:T(8,128)(2,1)}, u32[]{:S(2)}, u32[]{:S(2)}) collective-permute-start(bf16[2,128,656]{1,2,0:T(8,128)(2,1)} %constant_dynamic-slice_fusion.23), channel_id=1, source_target_pairs={{8,0},{12,4},{0,8},{4,12},{9,1},{13,5},{1,9},{5,13},{10,2},{14,6},... | collective-permute-start | bytes 1007624 | tf_op jit(solution)/shard_map/ppermute | solution.py:20
  122.8 30.5 %collective-permute-start.20 = (bf16[2,128,656]{1,2,0:T(8,128)(2,1)}, bf16[2,128,656]{1,2,0:T(8,128)(2,1)}, u32[]{:S(2)}, u32[]{:S(2)}) collective-permute-start(bf16[2,128,656]{1,2,0:T(8,128)(2,1)} %constant_dynamic-slice_fusion.23), channel_id=1, source_target_pairs={{12,0},{0,4},{4,8},{8,12},{13,1},{1,5},{5,9},{9,13},{14,2},{2,6},{... | collective-permute-start | bytes 1007624 | tf_op jit(solution)/shard_map/ppermute | solution.py:20
  155.5 27.5 %collective-permute-start.23 = (bf16[3,2,128,656]{2,3,1,0:T(8,128)(2,1)}, bf16[3,2,128,656]{2,3,1,0:T(8,128)(2,1)}, u32[]{:S(2)}, u32[]{:S(2)}) collective-permute-start(bf16[3,2,128,656]{2,3,1,0:T(8,128)(2,1)} %pad_maximum_fusion.11), channel_id=1, source_target_pairs={{0,16},{16,0},{1,17},{17,1},{2,18},{18,2},{3,19},{19,3},{4,20},{20... | collective-permute-start | bytes 3022856 | tf_op jit(solution)/shard_map/ppermute | solution.py:286
  162.9 16.6 %collective-permute-start.18 = (bf16[320,1024]{1,0:T(8,128)(2,1)}, bf16[320,1024]{1,0:T(8,128)(2,1)}, u32[]{:S(2)}, u32[]{:S(2)}) collective-permute-start(bf16[320,1024]{1,0:T(8,128)(2,1)} %add_convert_fusion.7), channel_id=1, source_target_pairs={{0,2},{1,3},{2,0},{3,1},{4,6},{5,7},{6,4},{7,5},{8,10},{9,11},{10,... | collective-permute-start | bytes 1966088 | tf_op jit(solution)/shard_map/ppermute | solution.py:286
  181.0 4.1 collective-permute-start.19
  199.0 4.9 collective-permute-start.27
  203.2 9.8 %collective-permute-start.24 = (bf16[320,1024]{1,0:T(8,128)(2,1)S(1)}, bf16[320,1024]{1,0:T(8,128)(2,1)S(1)}, u32[]{:S(2)}, u32[]{:S(2)}) collective-permute-start(bf16[320,1024]{1,0:T(8,128)(2,1)S(1)} %dynamic-slice_convert_fusion.2), channel_id=1, source_target_pairs={{0,1},{1,0},{2,3},{3,2},{4,5},{5,4},{6,7},{7,6},{8,9},{9,8},{10,11... | collective-permute-start | bytes 1966088 | tf_op jit(solution)/shard_map/ppermute | solution.py:286
  205.4 17.7 %collective-permute-start.28 = (bf16[320,1024]{1,0:T(8,128)(2,1)S(1)}, bf16[320,1024]{1,0:T(8,128)(2,1)S(1)}, u32[]{:S(2)}, u32[]{:S(2)}) collective-permute-start(bf16[320,1024]{1,0:T(8,128)(2,1)S(1)} %add_convert_fusion.3), channel_id=1, source_target_pairs={{0,2},{1,3},{2,0},{3,1},{4,6},{5,7},{6,4},{7,5},{8,10},{9,11},{10,... | collective-permute-start | bytes 1966088 | tf_op jit(solution)/shard_map/ppermute | solution.py:286
  213.3 22.7 %collective-permute-start.25 = (bf16[320,1024]{1,0:T(8,128)(2,1)S(1)}, bf16[320,1024]{1,0:T(8,128)(2,1)S(1)}, u32[]{:S(2)}, u32[]{:S(2)}) collective-permute-start(bf16[320,1024]{1,0:T(8,128)(2,1)S(1)} %add_convert_fusion.5), channel_id=1, source_target_pairs={{0,2},{1,3},{2,0},{3,1},{4,6},{5,7},{6,4},{7,5},{8,10},{9,11},{10,... | collective-permute-start | bytes 1966088 | tf_op jit(solution)/shard_map/ppermute | solution.py:286
  223.4 13.8 %collective-permute-start.29 = (bf16[320,1024]{1,0:T(8,128)(2,1)S(1)}, bf16[320,1024]{1,0:T(8,128)(2,1)S(1)}, u32[]{:S(2)}, u32[]{:S(2)}) collective-permute-start(bf16[320,1024]{1,0:T(8,128)(2,1)S(1)} %add_convert_fusion.2), channel_id=1, source_target_pairs={{0,1},{1,0},{2,3},{3,2},{4,5},{5,4},{6,7},{7,6},{8,9},{9,8},{10,11... | collective-permute-start | bytes 1966088 | tf_op jit(solution)/shard_map/ppermute | solution.py:286
  237.1 45.1 %collective-permute-start.26 = (bf16[320,1024]{1,0:T(8,128)(2,1)}, bf16[320,1024]{1,0:T(8,128)(2,1)}, u32[]{:S(2)}, u32[]{:S(2)}) collective-permute-start(bf16[320,1024]{1,0:T(8,128)(2,1)} %add_convert_fusion.4), channel_id=1, source_target_pairs={{0,1},{1,0},{2,3},{3,2},{4,5},{5,4},{6,7},{7,6},{8,9},{9,8},{10,11... | collective-permute-start | bytes 1966088 | tf_op jit(solution)/shard_map/ppermute | solution.py:286
  243.7 43.3 %collective-permute-start.32 = (bf16[1,64,640]{2,1,0:T(8,128)(2,1)}, bf16[1,64,640]{2,1,0:T(8,128)(2,1)S(1)}, u32[]{:S(2)}, u32[]{:S(2)}) collective-permute-start(bf16[1,64,640]{2,1,0:T(8,128)(2,1)} %get-tuple-element.123), channel_id=1, source_target_pairs={{4,0},{8,4},{12,8},{0,12},{5,1},{9,5},{13,9},{1,13},{6,2},{10,6},{... | collective-permute-start | bytes 245768 | tf_op jit(solution)/shard_map/ppermute | solution.py:20
  243.7 43.3 %collective-permute-start.31 = (bf16[1,64,640]{2,1,0:T(8,128)(2,1)}, bf16[1,64,640]{2,1,0:T(8,128)(2,1)S(1)}, u32[]{:S(2)}, u32[]{:S(2)}) collective-permute-start(bf16[1,64,640]{2,1,0:T(8,128)(2,1)} %get-tuple-element.122), channel_id=1, source_target_pairs={{8,0},{12,4},{0,8},{4,12},{9,1},{13,5},{1,9},{5,13},{10,2},{14,6},... | collective-permute-start | bytes 245768 | tf_op jit(solution)/shard_map/ppermute | solution.py:20
  246.4 40.6 %collective-permute-start.30 = (bf16[1,64,640]{2,1,0:T(8,128)(2,1)}, bf16[1,64,640]{2,1,0:T(8,128)(2,1)}, u32[]{:S(2)}, u32[]{:S(2)}) collective-permute-start(bf16[1,64,640]{2,1,0:T(8,128)(2,1)} %get-tuple-element.121), channel_id=1, source_target_pairs={{12,0},{0,4},{4,8},{8,12},{13,1},{1,5},{5,9},{9,13},{14,2},{2,6},{... | collective-permute-start | bytes 245768 | tf_op jit(solution)/shard_map/ppermute | solution.py:20
  263.1 166.0 %collective-permute-start.53 = (bf16[2,4,128,656]{2,3,1,0:T(8,128)(2,1)}, bf16[2,4,128,656]{2,3,1,0:T(8,128)(2,1)}, u32[]{:S(2)}, u32[]{:S(2)}) collective-permute-start(bf16[2,4,128,656]{2,3,1,0:T(8,128)(2,1)} %bitcast.466), channel_id=1, source_target_pairs={{0,16},{16,0},{1,17},{17,1},{2,18},{18,2},{3,19},{19,3},{4,20},{20... | collective-permute-start | bytes 4030472 | tf_op jit(solution)/shard_map/ppermute | solution.py:286
  282.2 112.1 %collective-permute-start.58 = (bf16[1,4,128,656]{2,3,1,0:T(8,128)(2,1)}, bf16[1,4,128,656]{2,3,1,0:T(8,128)(2,1)}, u32[]{:S(2)}, u32[]{:S(2)}) collective-permute-start(bf16[1,4,128,656]{2,3,1,0:T(8,128)(2,1)} %bitcast.467), channel_id=1, source_target_pairs={{0,16},{16,0},{1,17},{17,1},{2,18},{18,2},{3,19},{19,3},{4,20},{20... | collective-permute-start | bytes 2015240 | tf_op jit(solution)/shard_map/ppermute | solution.py:286
  318.3 9.8 %collective-permute-start.35 = (bf16[1,3,64,640]{3,2,1,0:T(8,128)(2,1)}, bf16[1,3,64,640]{3,2,1,0:T(8,128)(2,1)S(1)}, u32[]{:S(2)}, u32[]{:S(2)}) collective-permute-start(bf16[1,3,64,640]{3,2,1,0:T(8,128)(2,1)} %bitcast.518), channel_id=1, source_target_pairs={{4,0},{8,4},{12,8},{0,12},{5,1},{9,5},{13,9},{1,13},{6,2},{10,6},{... | collective-permute-start | bytes 737288 | tf_op jit(solution)/shard_map/ppermute | solution.py:20
  322.1 19.3 %collective-permute-start.34 = (bf16[1,3,64,640]{3,2,1,0:T(8,128)(2,1)}, bf16[1,3,64,640]{3,2,1,0:T(8,128)(2,1)}, u32[]{:S(2)}, u32[]{:S(2)}) collective-permute-start(bf16[1,3,64,640]{3,2,1,0:T(8,128)(2,1)} %bitcast.517), channel_id=1, source_target_pairs={{8,0},{12,4},{0,8},{4,12},{9,1},{13,5},{1,9},{5,13},{10,2},{14,6},... | collective-permute-start | bytes 737288 | tf_op jit(solution)/shard_map/ppermute | solution.py:20
  324.0 17.3 %collective-permute-start.33 = (bf16[1,3,64,640]{3,2,1,0:T(8,128)(2,1)}, bf16[1,3,64,640]{3,2,1,0:T(8,128)(2,1)}, u32[]{:S(2)}, u32[]{:S(2)}) collective-permute-start(bf16[1,3,64,640]{3,2,1,0:T(8,128)(2,1)} %bitcast.519), channel_id=1, source_target_pairs={{12,0},{0,4},{4,8},{8,12},{13,1},{1,5},{5,9},{9,13},{14,2},{2,6},{... | collective-permute-start | bytes 737288 | tf_op jit(solution)/shard_map/ppermute | solution.py:20
  328.1 44.1 %collective-permute-start.48 = (bf16[1,4,128,256]{3,2,1,0:T(8,128)(2,1)S(1)}, bf16[1,4,128,256]{3,2,1,0:T(8,128)(2,1)}, u32[]{:S(2)}, u32[]{:S(2)}) collective-permute-start(bf16[1,4,128,256]{3,2,1,0:T(8,128)(2,1)S(1)} %fusion.137), channel_id=1, source_target_pairs={{0,16},{16,0},{1,17},{17,1},{2,18},{18,2},{3,19},{19,3},{4,20},{20... | collective-permute-start | bytes 786440 | tf_op jit(solution)/shard_map/ppermute | solution.py:286
  375.7 6.9 %collective-permute-start.51 = (bf16[1,128,256]{1,2,0:T(8,128)(2,1)}, bf16[1,128,256]{1,2,0:T(8,128)(2,1)}, u32[]{:S(2)}, u32[]{:S(2)}) collective-permute-start(bf16[1,128,256]{1,2,0:T(8,128)(2,1)} %bitcast.529), channel_id=1, source_target_pairs={{4,0},{8,4},{12,8},{0,12},{5,1},{9,5},{13,9},{1,13},{6,2},{10,6},{... | collective-permute-start | bytes 196616 | tf_op jit(solution)/shard_map/ppermute | solution.py:20
  376.4 8.0 %collective-permute-start.50 = (bf16[1,128,256]{1,2,0:T(8,128)(2,1)}, bf16[1,128,256]{1,2,0:T(8,128)(2,1)}, u32[]{:S(2)}, u32[]{:S(2)}) collective-permute-start(bf16[1,128,256]{1,2,0:T(8,128)(2,1)} %bitcast.528), channel_id=1, source_target_pairs={{8,0},{12,4},{0,8},{4,12},{9,1},{13,5},{1,9},{5,13},{10,2},{14,6},... | collective-permute-start | bytes 196616 | tf_op jit(solution)/shard_map/ppermute | solution.py:20
  380.4 6.4 %collective-permute-start.49 = (bf16[1,128,256]{1,2,0:T(8,128)(2,1)}, bf16[1,128,256]{1,2,0:T(8,128)(2,1)}, u32[]{:S(2)}, u32[]{:S(2)}) collective-permute-start(bf16[1,128,256]{1,2,0:T(8,128)(2,1)} %bitcast.134), channel_id=1, source_target_pairs={{12,0},{0,4},{4,8},{8,12},{13,1},{1,5},{5,9},{9,13},{14,2},{2,6},{... | collective-permute-start | bytes 196616 | tf_op jit(solution)/shard_map/ppermute | solution.py:20
  382.6 29.9 %collective-permute-start.36 = (bf16[320,1024]{1,0:T(8,128)(2,1)}, bf16[320,1024]{1,0:T(8,128)(2,1)S(1)}, u32[]{:S(2)}, u32[]{:S(2)}) collective-permute-start(bf16[320,1024]{1,0:T(8,128)(2,1)} %dynamic-slice_convert_fusion), channel_id=1, source_target_pairs={{0,1},{1,0},{2,3},{3,2},{4,5},{5,4},{6,7},{7,6},{8,9},{9,8},{10,11... | collective-permute-start | bytes 1966088 | tf_op jit(solution)/shard_map/ppermute | solution.py:286
  387.8 10.1 %collective-permute-start.52 = (bf16[1,128,256]{1,2,0:T(8,128)(2,1)S(1)}, bf16[1,128,256]{1,2,0:T(8,128)(2,1)S(1)}, u32[]{:S(2)}, u32[]{:S(2)}) collective-permute-start(bf16[1,128,256]{1,2,0:T(8,128)(2,1)S(1)} %fusion.144), channel_id=1, source_target_pairs={{0,16},{16,0},{1,17},{17,1},{2,18},{18,2},{3,19},{19,3},{4,20},{20... | collective-permute-start | bytes 196616 | tf_op jit(solution)/shard_map/ppermute | solution.py:286
  396.0 16.4 %copy-start.36 = (f32[640,1024]{1,0:T(8,128)S(1)}, f32[640,1024]{1,0:T(8,128)}, u32[]{:S(2)}) copy-start(f32[640,1024]{1,0:T(8,128)} %convolution_bitcast_fusion.3) | copy-start | bytes 7864324
  396.1 6.4 %collective-permute-start.61 = (bf16[1,128,656]{1,2,0:T(8,128)(2,1)S(1)}, bf16[1,128,656]{1,2,0:T(8,128)(2,1)S(1)}, u32[]{:S(2)}, u32[]{:S(2)}) collective-permute-start(bf16[1,128,656]{1,2,0:T(8,128)(2,1)S(1)} %get-tuple-element.109), channel_id=1, source_target_pairs={{4,0},{8,4},{12,8},{0,12},{5,1},{9,5},{13,9},{1,13},{6,2},{10,6},{... | collective-permute-start | bytes 503816 | tf_op jit(solution)/shard_map/ppermute | solution.py:20
  397.0 15.0 %collective-permute-start.60 = (bf16[1,128,656]{1,2,0:T(8,128)(2,1)S(1)}, bf16[1,128,656]{1,2,0:T(8,128)(2,1)S(1)}, u32[]{:S(2)}, u32[]{:S(2)}) collective-permute-start(bf16[1,128,656]{1,2,0:T(8,128)(2,1)S(1)} %get-tuple-element.110), channel_id=1, source_target_pairs={{8,0},{12,4},{0,8},{4,12},{9,1},{13,5},{1,9},{5,13},{10,2},{14,6},... | collective-permute-start | bytes 503816 | tf_op jit(solution)/shard_map/ppermute | solution.py:20
  397.8 14.1 %collective-permute-start.59 = (bf16[1,128,656]{1,2,0:T(8,128)(2,1)S(1)}, bf16[1,128,656]{1,2,0:T(8,128)(2,1)S(1)}, u32[]{:S(2)}, u32[]{:S(2)}) collective-permute-start(bf16[1,128,656]{1,2,0:T(8,128)(2,1)S(1)} %get-tuple-element.108), channel_id=1, source_target_pairs={{12,0},{0,4},{4,8},{8,12},{13,1},{1,5},{5,9},{9,13},{14,2},{2,6},{... | collective-permute-start | bytes 503816 | tf_op jit(solution)/shard_map/ppermute | solution.py:20
  402.5 20.2 %collective-permute-start.43 = (bf16[3,4,128,256]{3,2,1,0:T(8,128)(2,1)S(1)}, bf16[3,4,128,256]{3,2,1,0:T(8,128)(2,1)S(1)}, u32[]{:S(2)}, u32[]{:S(2)}) collective-permute-start(bf16[3,4,128,256]{3,2,1,0:T(8,128)(2,1)S(1)} %bitcast.503), channel_id=1, source_target_pairs={{0,16},{16,0},{1,17},{17,1},{2,18},{18,2},{3,19},{19,3},{4,20},{20... | collective-permute-start | bytes 2359304 | tf_op jit(solution)/shard_map/ppermute | solution.py:286
  412.1 9.7 %collective-permute-start.62 = (bf16[1,128,656]{1,2,0:T(8,128)(2,1)S(1)}, bf16[1,128,656]{1,2,0:T(8,128)(2,1)S(1)}, u32[]{:S(2)}, u32[]{:S(2)}) collective-permute-start(bf16[1,128,656]{1,2,0:T(8,128)(2,1)S(1)} %fusion.135), channel_id=1, source_target_pairs={{0,16},{16,0},{1,17},{17,1},{2,18},{18,2},{3,19},{19,3},{4,20},{20... | collective-permute-start | bytes 503816 | tf_op jit(solution)/shard_map/ppermute | solution.py:286
  412.7 36.4 %collective-permute-start.37 = (bf16[320,1024]{1,0:T(8,128)(2,1)S(1)}, bf16[320,1024]{1,0:T(8,128)(2,1)S(1)}, u32[]{:S(2)}, u32[]{:S(2)}) collective-permute-start(bf16[320,1024]{1,0:T(8,128)(2,1)S(1)} %add_convert_fusion.1), channel_id=1, source_target_pairs={{0,2},{1,3},{2,0},{3,1},{4,6},{5,7},{6,4},{7,5},{8,10},{9,11},{10,... | collective-permute-start | bytes 1966088 | tf_op jit(solution)/shard_map/ppermute | solution.py:286
  422.9 13.1 %collective-permute-start.46 = (bf16[3,128,256]{2,1,0:T(8,128)(2,1)S(1)}, bf16[3,128,256]{2,1,0:T(8,128)(2,1)S(1)}, u32[]{:S(2)}, u32[]{:S(2)}) collective-permute-start(bf16[3,128,256]{2,1,0:T(8,128)(2,1)S(1)} %get-tuple-element.106), channel_id=1, source_target_pairs={{4,0},{8,4},{12,8},{0,12},{5,1},{9,5},{13,9},{1,13},{6,2},{10,6},{... | collective-permute-start | bytes 589832 | tf_op jit(solution)/shard_map/ppermute | solution.py:20
  426.7 22.0 %collective-permute-start.45 = (bf16[3,128,256]{2,1,0:T(8,128)(2,1)S(1)}, bf16[3,128,256]{2,1,0:T(8,128)(2,1)S(1)}, u32[]{:S(2)}, u32[]{:S(2)}) collective-permute-start(bf16[3,128,256]{2,1,0:T(8,128)(2,1)S(1)} %get-tuple-element.107), channel_id=1, source_target_pairs={{8,0},{12,4},{0,8},{4,12},{9,1},{13,5},{1,9},{5,13},{10,2},{14,6},... | collective-permute-start | bytes 589832 | tf_op jit(solution)/shard_map/ppermute | solution.py:20
  429.0 19.7 %collective-permute-start.44 = (bf16[3,128,256]{2,1,0:T(8,128)(2,1)S(1)}, bf16[3,128,256]{2,1,0:T(8,128)(2,1)S(1)}, u32[]{:S(2)}, u32[]{:S(2)}) collective-permute-start(bf16[3,128,256]{2,1,0:T(8,128)(2,1)S(1)} %get-tuple-element.105), channel_id=1, source_target_pairs={{12,0},{0,4},{4,8},{8,12},{13,1},{1,5},{5,9},{9,13},{14,2},{2,6},{... | collective-permute-start | bytes 589832 | tf_op jit(solution)/shard_map/ppermute | solution.py:20
  430.8 18.6 %collective-permute-start.56 = (bf16[2,128,656]{1,2,0:T(8,128)(2,1)S(1)}, bf16[2,128,656]{1,2,0:T(8,128)(2,1)S(1)}, u32[]{:S(2)}, u32[]{:S(2)}) collective-permute-start(bf16[2,128,656]{1,2,0:T(8,128)(2,1)S(1)} %get-tuple-element.70), channel_id=1, source_target_pairs={{4,0},{8,4},{12,8},{0,12},{5,1},{9,5},{13,9},{1,13},{6,2},{10,6},{... | collective-permute-start | bytes 1007624 | tf_op jit(solution)/shard_map/ppermute | solution.py:20
  436.0 32.9 %collective-permute-start.55 = (bf16[2,128,656]{1,2,0:T(8,128)(2,1)S(1)}, bf16[2,128,656]{1,2,0:T(8,128)(2,1)S(1)}, u32[]{:S(2)}, u32[]{:S(2)}) collective-permute-start(bf16[2,128,656]{1,2,0:T(8,128)(2,1)S(1)} %get-tuple-element.71), channel_id=1, source_target_pairs={{8,0},{12,4},{0,8},{4,12},{9,1},{13,5},{1,9},{5,13},{10,2},{14,6},... | collective-permute-start | bytes 1007624 | tf_op jit(solution)/shard_map/ppermute | solution.py:20
  448.7 20.1 %collective-permute-start.54 = (bf16[2,128,656]{1,2,0:T(8,128)(2,1)S(1)}, bf16[2,128,656]{1,2,0:T(8,128)(2,1)S(1)}, u32[]{:S(2)}, u32[]{:S(2)}) collective-permute-start(bf16[2,128,656]{1,2,0:T(8,128)(2,1)S(1)} %get-tuple-element.69), channel_id=1, source_target_pairs={{12,0},{0,4},{4,8},{8,12},{13,1},{1,5},{5,9},{9,13},{14,2},{2,6},{... | collective-permute-start | bytes 1007624 | tf_op jit(solution)/shard_map/ppermute | solution.py:20
  448.8 21.4 %collective-permute-start.47 = (bf16[3,128,256]{2,1,0:T(8,128)(2,1)S(1)}, bf16[3,128,256]{2,1,0:T(8,128)(2,1)S(1)}, u32[]{:S(2)}, u32[]{:S(2)}) collective-permute-start(bf16[3,128,256]{2,1,0:T(8,128)(2,1)S(1)} %fusion.132), channel_id=1, source_target_pairs={{0,16},{16,0},{1,17},{17,1},{2,18},{18,2},{3,19},{19,3},{4,20},{20... | collective-permute-start | bytes 589832 | tf_op jit(solution)/shard_map/ppermute | solution.py:286
  449.3 28.2 %collective-permute-start.38 = (bf16[320,1024]{1,0:T(8,128)(2,1)S(1)}, bf16[320,1024]{1,0:T(8,128)(2,1)S(1)}, u32[]{:S(2)}, u32[]{:S(2)}) collective-permute-start(bf16[320,1024]{1,0:T(8,128)(2,1)S(1)} %add_convert_fusion), channel_id=1, source_target_pairs={{0,1},{1,0},{2,3},{3,2},{4,5},{5,4},{6,7},{7,6},{8,9},{9,8},{10,11... | collective-permute-start | bytes 1966088 | tf_op jit(solution)/shard_map/ppermute | solution.py:286
  469.1 7.2 %collective-permute-start.57 = (bf16[2,128,656]{1,2,0:T(8,128)(2,1)S(1)}, bf16[2,128,656]{1,2,0:T(8,128)(2,1)S(1)}, u32[]{:S(2)}, u32[]{:S(2)}) collective-permute-start(bf16[2,128,656]{1,2,0:T(8,128)(2,1)S(1)} %fusion.123), channel_id=1, source_target_pairs={{0,16},{16,0},{1,17},{17,1},{2,18},{18,2},{3,19},{19,3},{4,20},{20... | collective-permute-start | bytes 1007624 | tf_op jit(solution)/shard_map/ppermute | solution.py:286
  478.9 5.7 %collective-permute-start.41 = (f32[2,256]{1,0:T(2,128)S(1)}, f32[2,256]{1,0:T(2,128)S(1)}, u32[]{:S(2)}, u32[]{:S(2)}) collective-permute-start(f32[2,256]{1,0:T(2,128)S(1)} %get-tuple-element.145), channel_id=1, source_target_pairs={{4,0},{8,4},{12,8},{0,12},{5,1},{9,5},{13,9},{1,13},{6,2},{10,6},{... | collective-permute-start | bytes 6152 | tf_op jit(solution)/shard_map/ppermute | solution.py:20
  478.9 5.6 %collective-permute-start.40 = (f32[2,256]{1,0:T(2,128)S(1)}, f32[2,256]{1,0:T(2,128)S(1)}, u32[]{:S(2)}, u32[]{:S(2)}) collective-permute-start(f32[2,256]{1,0:T(2,128)S(1)} %get-tuple-element.144), channel_id=1, source_target_pairs={{8,0},{12,4},{0,8},{4,12},{9,1},{13,5},{1,9},{5,13},{10,2},{14,6},... | collective-permute-start | bytes 6152 | tf_op jit(solution)/shard_map/ppermute | solution.py:20
  482.6 5.4 %collective-permute-start.39 = (f32[2,256]{1,0:T(2,128)S(1)}, f32[2,256]{1,0:T(2,128)S(1)}, u32[]{:S(2)}, u32[]{:S(2)}) collective-permute-start(f32[2,256]{1,0:T(2,128)S(1)} %get-tuple-element.143), channel_id=1, source_target_pairs={{12,0},{0,4},{4,8},{8,12},{13,1},{1,5},{5,9},{9,13},{14,2},{2,6},{... | collective-permute-start | bytes 6152 | tf_op jit(solution)/shard_map/ppermute | solution.py:20
  488.1 3.6 collective-permute-start.42
  (60 other events, 295.1 us)
